TPU v7x, 128 devices: a whole 4x4x4 slice. The times are simulated.
128 devices in a mesh: pipe: 2 (over core), ctx: 16 (over y, x), tp: 4 (over z).
Axes of the slice: x: 4, y: 4, z: 4, core: 2. Of those that a mesh axis runs over, the one named last changes fastest.
Arguments:
- queries: bfloat16 [2, 8192, 3584], P('pipe', ('ctx', 'tp')), may hold values from -20 to 20
- keys: bfloat16 [2, 8192, 3584], P('pipe', ('ctx', 'tp')), may hold values from -6 to 6
- values: bfloat16 [2, 8192, 3584], P('pipe', ('ctx', 'tp')), may hold values from -6 to 6
- out_grad: bfloat16 [2, 8192, 3584], P('pipe', ('ctx', 'tp')), may hold values from -6 to 6
- chosen: int32 [2, 16, 3], P('pipe'), may hold values from 0 to 14, as said below
Outputs:
- out_next: bfloat16 [2, 8192, 3584], P('pipe', ('ctx', 'tp'))
- query_back: bfloat16 [2, 8192, 3584], P('pipe', ('ctx', 'tp'))
- key_back: bfloat16 [2, 8192, 3584], P('pipe', ('ctx', 'tp'))
- value_back: bfloat16 [2, 8192, 3584], P('pipe', ('ctx', 'tp'))
Inputs may be any that keep to these rules, and one draw needn't show every extreme that they name: chosen[s, i, j] is at most i; its entries below i are distinct, there are min(i, 3) of them and the others equal i; block i - 1 is always among them; earlier blocks are chosen more often.
All inputs are finite; a program needn't handle non-finite values.
Results may differ from a plain program's by a relative error of at most 0.0056.
Values may be sent and summed in bfloat16 or wider, within the bound.
No kernel may reach another device: no remote copies, remote signals or barrier semaphores. Data moves between devices by JAX's collectives and lax.ppermute only.
A program may use at most 384 MiB of HBM per device.

v0:
```python
import math

import jax
import jax.numpy as jnp
from jax import lax
from jax.sharding import PartitionSpec as P

HD = 128
BLK = 512
TOPK = 3


def shifted(value, axis, steps):
    count = lax.axis_size(axis)
    initial, last = (max(0, -steps), min(count, count - steps))
    return lax.ppermute(value, axis, [(source, source + steps) for source in range(initial, last)])


def slot_mask(picked, block, size, count):
    rows = lax.broadcasted_iota(jnp.int32, (size, size), 0)
    cols = lax.broadcasted_iota(jnp.int32, (size, size), 1)
    parts = [jnp.broadcast_to(picked[j] < block, (size, size)) for j in range(count)]
    parts.append(cols <= rows)
    return jnp.concatenate(parts, axis=1)


def head_forward(query, keyset, valueset, valid):
    scale = 1.0 / math.sqrt(query.shape[-1])
    scores = jnp.einsum("qd,kd->qk", query, keyset, preferred_element_type=jnp.float32) * scale
    scores = jnp.where(valid, scores, -jnp.inf)
    top = jnp.max(scores, axis=-1, keepdims=True)
    total = jnp.log(jnp.sum(jnp.exp(scores - top), axis=-1, keepdims=True)) + top
    probs = jnp.exp(scores - total).astype(jnp.bfloat16)
    attended = jnp.einsum("qk,kd->qd", probs, valueset, preferred_element_type=jnp.float32).astype(
        jnp.bfloat16
    )
    return (attended, total)


def head_backward(query, keyset, valueset, grad, attended, total, valid):
    scale = 1.0 / math.sqrt(query.shape[-1])
    scores = jnp.einsum("qd,kd->qk", query, keyset, preferred_element_type=jnp.float32) * scale
    scores = jnp.where(valid, scores, -jnp.inf)
    probs = jnp.exp(scores - total)
    low = probs.astype(jnp.bfloat16)
    value_part = jnp.einsum("qk,qd->kd", low, grad, preferred_element_type=jnp.float32)
    prob_grad = jnp.einsum("qd,kd->qk", grad, valueset, preferred_element_type=jnp.float32)
    delta = jnp.sum(grad.astype(jnp.float32) * attended.astype(jnp.float32), axis=-1, keepdims=True)
    score_grad = (probs * (prob_grad - delta)).astype(jnp.bfloat16)
    query_part = (
        jnp.einsum("qk,kd->qd", score_grad, keyset, preferred_element_type=jnp.float32) * scale
    ).astype(jnp.bfloat16)
    key_part = (
        jnp.einsum("qk,qd->kd", score_grad, query, preferred_element_type=jnp.float32) * scale
    )
    return (query_part, key_part, value_part)


def split_heads(array):
    return array.reshape(array.shape[0], -1, HD).transpose(1, 0, 2)


def join_heads(array):
    return array.transpose(1, 0, 2).reshape(array.shape[1], -1)


def pick_slots(whole, blocks, size):
    return jnp.concatenate(
        [
            lax.dynamic_slice_in_dim(whole, blocks[j] * size, size, 0)
            for j in range(blocks.shape[0])
        ],
        axis=0,
    )


def on_device(queries, keys, values, out_grad, chosen):
    q_heads, k_heads, v_heads, g_heads = (
        lax.all_to_all(queries, "tp", split_axis=2, concat_axis=1, tiled=True),
        lax.all_to_all(keys, "tp", split_axis=2, concat_axis=1, tiled=True),
        lax.all_to_all(values, "tp", split_axis=2, concat_axis=1, tiled=True),
        lax.all_to_all(out_grad, "tp", split_axis=2, concat_axis=1, tiled=True),
    )
    rows = q_heads.shape[1]
    local = rows // BLK
    ctx_at = lax.axis_index("ctx")
    whole_keys, whole_values = (
        lax.all_gather(k_heads, "ctx", axis=1, tiled=True),
        lax.all_gather(v_heads, "ctx", axis=1, tiled=True),
    )
    own_key_terms = []
    own_value_terms = []
    total_rows = []
    delta_rows = []
    block = ctx_at * local + 0
    picked = chosen[0, block]
    blocks = jnp.concatenate([picked, block[None]])
    valid = slot_mask(picked, block, BLK, TOPK)
    query = split_heads(q_heads[0, 0:BLK])
    grad = split_heads(g_heads[0, 0:BLK])
    keyset = split_heads(pick_slots(whole_keys[0], blocks, BLK))
    valueset = split_heads(pick_slots(whole_values[0], blocks, BLK))
    attended, total = lax.map(
        lambda items: head_forward(items[0], items[1], items[2], valid), (query, keyset, valueset)
    )
    query_part, key_part, value_part = lax.map(
        lambda items: head_backward(
            items[0], items[1], items[2], items[3], items[4], items[5], valid
        ),
        (query, keyset, valueset, grad, attended, total),
    )
    delta = jnp.sum(grad.astype(jnp.float32) * attended.astype(jnp.float32), axis=-1)
    attended_parts = join_heads(attended)
    query_parts = join_heads(query_part)
    slot_terms = (blocks, jnp.concatenate([join_heads(key_part), join_heads(value_part)], axis=1))
    own_key_terms.append(key_part[:, TOPK * BLK :])
    own_value_terms.append(value_part[:, TOPK * BLK :])
    total_rows.append(total[:, :, 0].T)
    delta_rows.append(delta.T)
    attended_local = attended_parts
    features = attended_local.shape[1]
    padded = jnp.zeros((lax.axis_size("ctx") * rows + 2 * BLK, 2 * features), jnp.float32)
    blocks, terms = slot_terms
    for slot in range(TOPK + 1):
        place = jnp.clip(blocks[slot] * BLK + BLK, 0, lax.axis_size("ctx") * rows + BLK)
        piece = lax.dynamic_slice_in_dim(terms, slot * BLK, BLK, 0)
        current = lax.dynamic_slice_in_dim(padded, place, BLK, 0)
        padded = lax.dynamic_update_slice_in_dim(padded, current + piece, place, 0)
    owned = lax.psum_scatter(
        padded[BLK : BLK + lax.axis_size("ctx") * rows], "ctx", scatter_dimension=0, tiled=True
    )
    key_local = owned[:, :features].astype(jnp.bfloat16)
    value_local = owned[:, features:].astype(jnp.bfloat16)
    attended_local = attended_local[None]
    stacked = jnp.stack([query_parts, key_local, value_local])[:, None]
    out_tokens = lax.all_to_all(attended_local, "tp", split_axis=1, concat_axis=2, tiled=True)
    out_next = shifted(out_tokens, "pipe", 1)
    grad_tokens = lax.all_to_all(stacked, "tp", split_axis=2, concat_axis=3, tiled=True)
    moved = shifted(grad_tokens, "pipe", -1)
    return (out_next, moved[0], moved[1], moved[2])


def solution(mesh):
    placed = (
        P("pipe", ("ctx", "tp"), None),
        P("pipe", ("ctx", "tp"), None),
        P("pipe", ("ctx", "tp"), None),
        P("pipe", ("ctx", "tp"), None),
        P("pipe", None, None),
    )
    return jax.shard_map(
        on_device,
        mesh=mesh,
        in_specs=placed,
        out_specs=(
            P("pipe", ("ctx", "tp"), None),
            P("pipe", ("ctx", "tp"), None),
            P("pipe", ("ctx", "tp"), None),
            P("pipe", ("ctx", "tp"), None),
        ),
        check_vma=False,
    )
```

profile of v0, /device:TPU:1, one launch (start us, length us, event | category | flops | bytes accessed | tf_op | source)
XLA Modules:
  0.0 1031.6 jit_solution(11340079907337238892)
XLA Ops:
  7.2 4.3 copy.103
  12.0 19.6 %reduce.2 = bf16[3584,128]{1,0:T(8,128)(2,1)S(1)} reduce(bf16[3584,1,128]{2,1,0:T(2,128)(2,1)S(1)} %bitcast.180, bf16[]{:T(256)} %broadcast.32), dimensions={1}, to_apply=%bitcast.117.reduce_sub_computation | reduce | bytes 1835010
  32.0 18.4 %all_to_all.102 = bf16[4,2,57344]{2,1,0:T(2,128)(2,1)S(1)} all-to-all(bf16[4,2,57344]{2,1,0:T(2,128)(2,1)S(1)} %reshape.82), channel_id=1, replica_groups=mesh['pipe'=2,'ctx'=16,'tp'=4] {'tp'}, dimensions={0} | all-to-all | bytes 1835008 | tf_op jit(solution)/shard_map/all_to_all | solution.py:80
  52.7 4.3 copy.109
  57.0 19.6 %reduce.1 = bf16[3584,128]{1,0:T(8,128)(2,1)S(1)} reduce(bf16[3584,1,128]{2,1,0:T(2,128)(2,1)S(1)} %bitcast.187, bf16[]{:T(256)} %broadcast.32), dimensions={1}, to_apply=%bitcast.119.reduce_sub_computation | reduce | bytes 1835010
  77.0 14.4 %all_to_all.103 = bf16[4,2,57344]{2,1,0:T(2,128)(2,1)S(1)} all-to-all(bf16[4,2,57344]{2,1,0:T(2,128)(2,1)S(1)} %reshape.84), channel_id=1, replica_groups=mesh['pipe'=2,'ctx'=16,'tp'=4] {'tp'}, dimensions={0} | all-to-all | bytes 1835008 | tf_op jit(solution)/shard_map/all_to_all | solution.py:81
  93.7 4.3 copy.101
  98.0 19.6 %reduce = bf16[3584,128]{1,0:T(8,128)(2,1)S(1)} reduce(bf16[3584,1,128]{2,1,0:T(2,128)(2,1)S(1)} %bitcast.188, bf16[]{:T(256)} %broadcast.32), dimensions={1}, to_apply=%bitcast.115.reduce_sub_computation | reduce | bytes 1835010
  128.1 4.3 copy.121
  132.4 19.6 %reduce.4 = bf16[3584,128]{1,0:T(8,128)(2,1)S(1)} reduce(bf16[3584,1,128]{2,1,0:T(2,128)(2,1)S(1)} %bitcast.189, bf16[]{:T(256)} %broadcast.32), dimensions={1}, to_apply=%bitcast.123.reduce_sub_computation | reduce | bytes 1835010
  163.7 4.4 all-to-all-done.4
  172.9 84.1 %all-gather.5.cloned.1.call-done = bf16[1,8192,896]{2,1,0:T(8,128)(2,1)} async-done(((bf16[1,512,896]{2,1,0:T(8,128)(2,1)}), bf16[1,8192,896]{2,1,0:T(8,128)(2,1)}) %all-gather.5.cloned.1.call-update) | async-done | bytes 14680080 | tf_op jit(solution)/shard_map/all_gather | solution.py:89
  256.9 6.3 constant_dynamic-slice_fusion.9
  272.8 6.1 copy.117
  288.5 6.1 copy.116
  294.6 36.9 %while.26 = (s32[]{:T(128)}, bf16[7,512,128]{2,1,0:T(8,128)(2,1)}, f32[7,512,1]{1,2,0:T(1,128)S(1)}, bf16[7,512,128]{2,1,0:T(8,128)(2,1)}, bf16[7,2048,128]{2,1,...) while((s32[]{:T(128)}, bf16[7,512,128]{2,1,0:T(8,128)(2,1)}, ...), condition=%wide.region_3.4_spmd, body=%wide.region_0.3_spmd.sunk | while | flops 544275968 | bytes 14962785 | solution.py:103
  331.5 114.9 %while.27 = (s32[]{:T(128)}, bf16[7,512,128]{1,2,0:T(8,128)(2,1)}, f32[7,2048,128]{1,2,0:T(8,128)}, f32[7,2048,128]{1,2,0:T(8,128)}, bf16[7,512,128]{2,1,0:T(8,1...) while((s32[]{:T(128)}, bf16[7,512,128]{1,2,0:T(8,128)(2,1)}, ...), condition=%wide.region_6.7_spmd, body=%wide.region_4.6_spmd.sunk | while | flops 1350172160 | bytes 46544052 | solution.py:106
  450.6 20.9 %broadcast_in_dim.48 = f32[9216,1792]{0,1:T(8,128)} broadcast(f32[]{:T(128)} %constant.72.clone.1), dimensions={} | broadcast | bytes 66060292 | tf_op jit(solution)/shard_map/broadcast_in_dim | solution.py:122
  471.5 18.3 %dynamic_update_slice.30 = f32[9216,1792]{0,1:T(8,128)} dynamic-update-slice(f32[9216,1792]{0,1:T(8,128)} %broadcast_in_dim.48, f32[512,1792]{0,1:T(8,128)} %fusion.37, s32[]{:T(128)S(6)} %min.13, s32[]{:T(128)} %constant.70.clone.1) | dynamic-update-slice | bytes 7340036 | tf_op jit(solution)/shard_map/dynamic_update_slice | solution.py:128
  489.9 6.3 fusion.39
  496.1 18.3 %dynamic_update_slice.31 = f32[9216,1792]{0,1:T(8,128)} dynamic-update-slice(f32[9216,1792]{0,1:T(8,128)} %dynamic_update_slice.30, f32[512,1792]{0,1:T(8,128)} %fusion.39, s32[]{:T(128)S(6)} %min.14, s32[]{:T(128)} %constant.70.clone.1) | dynamic-update-slice | bytes 7340036 | tf_op jit(solution)/shard_map/dynamic_update_slice | solution.py:128
  514.4 6.3 fusion.36
  520.7 18.3 %dynamic_update_slice.32 = f32[9216,1792]{0,1:T(8,128)} dynamic-update-slice(f32[9216,1792]{0,1:T(8,128)} %dynamic_update_slice.31, f32[512,1792]{0,1:T(8,128)} %fusion.36, s32[]{:T(128)S(6)} %min.15, s32[]{:T(128)} %constant.70.clone.1) | dynamic-update-slice | bytes 7340036 | tf_op jit(solution)/shard_map/dynamic_update_slice | solution.py:128
  539.0 6.3 fusion.40
  545.3 18.3 %dynamic_update_slice.33 = f32[9216,1792]{0,1:T(8,128)} dynamic-update-slice(f32[9216,1792]{0,1:T(8,128)} %dynamic_update_slice.32, f32[512,1792]{0,1:T(8,128)} %fusion.40, s32[]{:T(128)S(6)} %min.16, s32[]{:T(128)} %constant.70.clone.1) | dynamic-update-slice | bytes 7340036 | tf_op jit(solution)/shard_map/dynamic_update_slice | solution.py:128
  563.6 39.1 %slice.50 = f32[8192,1792]{0,1:T(8,128)} slice(f32[9216,1792]{0,1:T(8,128)} %dynamic_update_slice.33), slice={[512:8704], [0:1792]} | slice | bytes 117440512 | tf_op jit(solution)/shard_map/slice | solution.py:130
  602.7 321.5 %reduce-scatter.2.cloned.1.call-done = f32[512,1792]{0,1:T(8,128)} async-done(((f32[8192,1792]{0,1:T(8,128)}), f32[512,1792]{0,1:T(8,128)}) %reduce-scatter.2.cloned.1.call-update) | async-done | bytes 3670032 | tf_op jit(solution)/shard_map/reduce_scatter | solution.py:129
  927.0 4.7 copy.130
  931.7 46.5 %all_to_all.104 = bf16[3,1,512,896]{3,0,1,2:T(4,128)(2,1)S(1)} all-to-all(bf16[3,1,512,896]{3,0,1,2:T(4,128)(2,1)} %copy.130), channel_id=1, replica_groups=mesh['pipe'=2,'ctx'=16,'tp'=4] {'tp'}, dimensions={2} | all-to-all | bytes 5505024 | tf_op jit(solution)/shard_map/all_to_all | solution.py:138
  981.2 5.3 collective-permute-start.1
  990.7 6.2 reduce.3
  997.2 14.7 %all_to_all.105 = bf16[4,2,57344]{2,1,0:T(2,128)(2,1)S(1)} all-to-all(bf16[4,2,57344]{2,1,0:T(2,128)(2,1)S(1)} %reshape.86), channel_id=1, replica_groups=mesh['pipe'=2,'ctx'=16,'tp'=4] {'tp'}, dimensions={0} | all-to-all | bytes 1835008 | tf_op jit(solution)/shard_map/all_to_all | solution.py:136
  (218 shorter events, 226.1 us)
Async XLA Ops:
  7.2 165.7 %all-gather.3.cloned.1.call-start = ((), (), s32[]{:S(2)}) async-start(), calls=%async_computation.7 | async-start | bytes 15597568 | tf_op jit(solution)/shard_map/all_gather | solution.py:88
  52.7 204.2 %all-gather.5.cloned.1.call-start = ((), (), s32[]{:S(2)}) async-start(), calls=%async_computation.8 | async-start | bytes 15597568 | tf_op jit(solution)/shard_map/all_gather | solution.py:89
  93.7 29.8 %copy-start.3 = (s32[1,16,3]{1,0,2:T(1,128)S(1)}, s32[1,16,3]{1,0,2:T(1,128)}, u32[]{:S(2)}) copy-start(s32[1,16,3]{1,0,2:T(1,128)} %param.13) | copy-start | bytes 580
  119.2 34.4 %all-to-all-start = ((bf16[4,2,57344]{2,1,0:T(2,128)(2,1)}), bf16[4,2,57344]{2,1,0:T(2,128)(2,1)}, u32[]{:S(2)}, u32[]{:S(2)}) async-start(bf16[4,2,57344]{2,1,0:T(2,128)(2,1)} %reshape.80), calls=%async_computation | async-start | bytes 1835008 | tf_op jit(solution)/shard_map/all_to_all | solution.py:79
  153.7 14.4 %all-to-all-start.4 = ((bf16[4,2,57344]{2,1,0:T(2,128)(2,1)}), bf16[4,2,57344]{2,1,0:T(2,128)(2,1)}, u32[]{:S(2)}, u32[]{:S(2)}) async-start(bf16[4,2,57344]{2,1,0:T(2,128)(2,1)} %reshape.88), calls=%async_computation.4 | async-start | bytes 1835008 | tf_op jit(solution)/shard_map/all_to_all | solution.py:82
  157.9 766.3 %reduce-scatter.2.cloned.1.call-start = ((), (), s32[]{:S(2)}) async-start(), calls=%async_computation.9 | async-start | bytes 62390272 | tf_op jit(solution)/shard_map/reduce_scatter | solution.py:129
  272.8 6.1 copy-start.1
  336.3 4.4 copy-start
  352.6 4.4 copy-start
  368.9 4.4 copy-start
  385.3 4.4 copy-start
  401.7 4.4 copy-start
  418.0 4.4 copy-start
  434.3 4.4 copy-start
  924.2 2.5 copy-start.2
  981.2 37.9 %collective-permute-start.1 = (bf16[3,1,128,3584]{2,3,0,1:T(8,128)(2,1)}, bf16[3,1,128,3584]{2,3,0,1:T(8,128)(2,1)}, u32[]{:S(2)}, u32[]{:S(2)}) collective-permute-start(bf16[3,1,128,3584]{2,3,0,1:T(8,128)(2,1)} %bitcast.207), channel_id=1, source_target_pairs={{64,0},{65,1},{66,2},{67,3},{68,4},{69,5},{70,6},{71,7},{72,8},{73... | collective-permute-start | bytes 8257544 | tf_op jit(solution)/shard_map/ppermute | solution.py:16
  1013.5 4.4 collective-permute-start
Sparse Core Ops, SparseCore 0:
  52.8 101.1 all-gather.2
  156.7 100.1 all-gather.4
  602.8 321.3 reduce-scatter.1
where the time goes:
time: 1040 us; the launch traced here: 1030 us
  waiting for transfers between devices  413 us (40%)
  local copies, waits for them, and re-layouts  244 us (23%)
  other arithmetic  130 us (12%)
  matrix products  116 us (11%)
  blocking collectives  94 us (9%)
  between operations  18.2 us (2%)
  starting transfers between devices  15.4 us (1%)
    reduce_scatter x1, waiting for transfers between devices, on_device(): lax.psum_scatter(padded[BLK:BLK + lax.axis_size('ctx') * rows], 'ctx', sc...  322 us
    unnamed x5, other arithmetic  84.8 us
    all_gather x1, waiting for transfers between devices, on_device(): lax.all_gather(v_heads, 'ctx', axis=1, tiled=True)  84.1 us
    dynamic_update_slice x4, local copies, waits for them, and re-layouts, on_device(): padded = lax.dynamic_update_slice_in_dim(padded, current + piece, place, 0)  73.2 us
    all_to_all x1, blocking collectives, on_device(): lax.all_to_all(stacked, 'tp', split_axis=2, concat_axis=3, tiled=True)  46.5 us
    slice x1, local copies, waits for them, and re-layouts, on_device(): padded[BLK:BLK + lax.axis_size('ctx') * rows]  39.1 us
    unnamed x30, local copies, waits for them, and re-layouts  35.1 us
    dot_general x7, matrix products, head_backward(): jnp.einsum('qk,qd->kd', low, grad, preferred_element_type=jnp.float32)  26 us
  transfers between devices with their start and end apart: 7, of which 4 were waited for; matrix products, arithmetic and copies ran while one was open for 10% of the time, Pallas kernels for 0%

commit v1 on v0

v1 whole, which is shorter than its diff:
```python
import math

import jax
import jax.numpy as jnp
from jax import lax
from jax.experimental import pallas as pl
from jax.experimental.pallas import tpu as pltpu
from jax.sharding import PartitionSpec as P

HD = 128
BLK = 512
TOPK = 3
HALF = 64
PART = 4
ROWS = PART * HALF
WIDE = 32
STEP = 4
VMEM = 56 * 1024 * 1024

BF = jnp.bfloat16
F32 = jnp.float32


def dot(a, b, dims):
    return lax.dot_general(a, b, (dims, ((), ())), preferred_element_type=F32)


NN = ((1,), (0,))


def spread_kernel(k_ref, v_ref, q_ref, g_ref, out_ref):
    for a, ref in enumerate((k_ref, v_ref, q_ref, g_ref)):
        for h in range(STEP):
            for half in range(2):
                out_ref[half, h, a] = ref[0, half * HALF : (half + 1) * HALF, h * HD : (h + 1) * HD]


def spread(keys, values, queries, grads):
    heads = keys.shape[2] // HD
    item = pl.BlockSpec((1, 2 * HALF, STEP * HD), lambda i: (0, 0, i))
    return pl.pallas_call(
        spread_kernel,
        grid=(heads // STEP,),
        in_specs=[item] * 4,
        out_specs=pl.BlockSpec((2, STEP, 4, HALF, HD), lambda i: (0, i, 0, 0, 0)),
        out_shape=jax.ShapeDtypeStruct((2, WIDE, 4, HALF, HD), BF),
        compiler_params=pltpu.CompilerParams(vmem_limit_bytes=VMEM),
        name="spread_heads",
    )(keys, values, queries, grads)


def attend_kernel(
    place_ref, picks_ref, own_ref, other_ref,
    first_ref, mine_ref, theirs_ref,
    kt_ref, vt_ref, s_ref, sum_ref,
):
    nb = picks_ref.shape[0]
    core, seg = place_ref[0], place_ref[1]
    scale = 1.0 / math.sqrt(HD)
    power = scale * math.log2(math.e)

    def part(a, half, b):
        ref = own_ref if half == 0 else other_ref
        return ref[pl.ds(b * PART, PART), a].reshape(ROWS, HD)

    def turn(b, carry):
        for half in range(2):
            kt_ref[half * nb + b] = part(0, half, b).T
            vt_ref[half * nb + b] = part(1, half, b).T
        for a in range(2):
            mine_ref[a, pl.ds(b * PART, PART)] = jnp.zeros((PART, HALF, HD), F32)
            sum_ref[a, pl.ds(b * PART, PART)] = jnp.zeros((PART, HALF, HD), F32)
        return carry

    lax.fori_loop(0, nb, turn, 0)

    def one_block(i, carry):
        q = part(2, 0, i)
        g = part(3, 0, i)
        qt = q.T
        gt = g.T
        slots = [picks_ref[i, j] for j in range(TOPK)] + [i]
        chunks = [(j, half) for j in range(TOPK + 1) for half in range(2)]
        key_at = lax.broadcasted_iota(jnp.int32, (ROWS, ROWS), 0)
        query_at = lax.broadcasted_iota(jnp.int32, (ROWS, ROWS), 1)
        top = jnp.full((1, ROWS), -jnp.inf, F32)
        for n, (j, half) in enumerate(chunks):
            s = dot(part(0, half, slots[j]), qt, NN)
            if j < TOPK:
                valid = slots[j] < i
            elif half == 0:
                valid = key_at <= query_at
            else:
                valid = key_at // HALF < query_at // HALF + core
            s = jnp.where(valid, s, -jnp.inf)
            s_ref[n] = s
            top = jnp.maximum(top, jnp.max(s, axis=0, keepdims=True))
        total = jnp.zeros((1, ROWS), F32)
        for n in range(len(chunks)):
            e = jnp.exp2((s_ref[n] - top) * power)
            s_ref[n] = e
            total = total + jnp.sum(e, axis=0, keepdims=True)
        inverse = 1.0 / total
        out_t = jnp.zeros((HD, ROWS), F32)
        for n, (j, half) in enumerate(chunks):
            p = s_ref[n] * inverse
            low = p.astype(BF)
            s_ref[n] = p
            out_t = out_t + dot(vt_ref[half * nb + slots[j]], low, NN)
            at = pl.ds(slots[j] * PART, PART)
            acc = mine_ref if half == 0 else sum_ref
            acc[1, at] += dot(low, g, NN).reshape(PART, HALF, HD)
        out = out_t.T.astype(BF)
        delta = jnp.sum(gt.astype(F32) * out_t.astype(BF).astype(F32), axis=0, keepdims=True)
        query_t = jnp.zeros((HD, ROWS), F32)
        for n, (j, half) in enumerate(chunks):
            dp = dot(part(1, half, slots[j]), gt, NN)
            ds = (s_ref[n] * (dp - delta)).astype(BF)
            query_t = query_t + dot(kt_ref[half * nb + slots[j]], ds, NN)
            at = pl.ds(slots[j] * PART, PART)
            acc = mine_ref if half == 0 else sum_ref
            acc[0, at] += dot(ds, q, NN).reshape(PART, HALF, HD)
        query = (query_t * scale).T.astype(BF)
        first = jnp.where(seg == 0, out.astype(F32), query.astype(F32)).astype(BF)
        first_ref[pl.ds(i * PART, PART)] = first.reshape(PART, HALF, HD)
        return carry

    lax.fori_loop(0, nb, one_block, 0)

    def finish(b, carry):
        for a in range(2):
            at = pl.ds(b * PART, PART)
            theirs_ref[a, at] = sum_ref[a, at].astype(theirs_ref.dtype)
        return carry

    lax.fori_loop(0, nb, finish, 0)


def attend(place, picks, own, other):
    nb = picks.shape[0]
    n = nb * PART
    smem = pl.BlockSpec(memory_space=pltpu.SMEM)
    vmem = pl.BlockSpec(memory_space=pltpu.VMEM)
    work = 6 * 2 * nb * ROWS * (TOPK + 1) * BLK * HD
    return pl.pallas_call(
        attend_kernel,
        in_specs=[smem, smem, vmem, vmem],
        out_specs=[vmem, vmem, vmem],
        out_shape=[
            jax.ShapeDtypeStruct((n, HALF, HD), BF),
            jax.ShapeDtypeStruct((2, n, HALF, HD), F32),
            jax.ShapeDtypeStruct((2, n, HALF, HD), BF),
        ],
        scratch_shapes=[
            pltpu.VMEM((2 * nb, HD, ROWS), BF),
            pltpu.VMEM((2 * nb, HD, ROWS), BF),
            pltpu.VMEM((2 * (TOPK + 1), ROWS, ROWS), F32),
            pltpu.VMEM((2, n, HALF, HD), F32),
        ],
        compiler_params=pltpu.CompilerParams(vmem_limit_bytes=VMEM),
        cost_estimate=pl.CostEstimate(flops=work, bytes_accessed=20 << 20, transcendentals=0),
        name="attend_head",
    )(place, picks, own, other)


def combine_kernel(first_ref, mine_ref, got_ref, out_ref):
    scale = 1.0 / math.sqrt(HD)
    out_ref[:, 0] = first_ref[...]
    out_ref[:, 1] = ((mine_ref[0] + got_ref[0].astype(F32)) * scale).astype(BF)
    out_ref[:, 2] = (mine_ref[1] + got_ref[1].astype(F32)).astype(BF)


def combine(first, mine, got):
    n = first.shape[0]
    size = n // 4
    return pl.pallas_call(
        combine_kernel,
        grid=(4,),
        in_specs=[
            pl.BlockSpec((size, HALF, HD), lambda i: (i, 0, 0)),
            pl.BlockSpec((2, size, HALF, HD), lambda i: (0, i, 0, 0)),
            pl.BlockSpec((2, size, HALF, HD), lambda i: (0, i, 0, 0)),
        ],
        out_specs=pl.BlockSpec((size, 3, HALF, HD), lambda i: (i, 0, 0, 0)),
        out_shape=jax.ShapeDtypeStruct((n, 3, HALF, HD), BF),
        compiler_params=pltpu.CompilerParams(vmem_limit_bytes=VMEM),
        name="combine_halves",
    )(first, mine, got)


def gather_kernel(place_ref, ao_ref, ag_ref, bo_ref, bg_ref, o_ref, dq_ref, dk_ref, dv_ref):
    core = place_ref[0]

    def fill(ref, own, got, live):
        for h in range(STEP):
            for half in range(2):
                value = jnp.where(core == half, own(h), got(h))
                value = jnp.where(live, value, jnp.zeros_like(value))
                ref[0, half * HALF : (half + 1) * HALF, h * HD : (h + 1) * HD] = value

    fill(o_ref, lambda h: ao_ref[h, 0], lambda h: bo_ref[h], core == 1)
    for a, ref in enumerate((dq_ref, dk_ref, dv_ref)):
        fill(ref, lambda h: ag_ref[h, a], lambda h: bg_ref[h, a], core == 0)


def gather(place, whole, got_out, got_grads, heads):
    item = pl.BlockSpec((1, 2 * HALF, STEP * HD), lambda i: (0, 0, i))
    shape = jax.ShapeDtypeStruct((1, 2 * HALF, heads * HD), BF)
    return pl.pallas_call(
        gather_kernel,
        grid=(heads // STEP,),
        in_specs=[
            pl.BlockSpec(memory_space=pltpu.SMEM),
            pl.BlockSpec((STEP, 1, HALF, HD), lambda i: (i, 0, 0, 0)),
            pl.BlockSpec((STEP, 3, HALF, HD), lambda i: (WIDE // STEP + i, 0, 0, 0)),
            pl.BlockSpec((STEP, HALF, HD), lambda i: (i, 0, 0)),
            pl.BlockSpec((STEP, 3, HALF, HD), lambda i: (i, 0, 0, 0)),
        ],
        out_specs=[item] * 4,
        out_shape=[shape] * 4,
        compiler_params=pltpu.CompilerParams(vmem_limit_bytes=VMEM),
        name="gather_heads",
    )(place, whole, whole, got_out, got_grads)


CHIPS = ("ctx", "tp")
SWAP = [(0, 1), (1, 0)]


def on_device(queries, keys, values, out_grad, chosen):
    heads = queries.shape[2] // HD
    core = lax.axis_index("pipe")
    seg = lax.axis_index(CHIPS) // WIDE
    place = jnp.stack([core, seg]).astype(jnp.int32)
    picks = jnp.where(seg == core, chosen, lax.ppermute(chosen, "pipe", SWAP))[0]

    parts = lax.all_to_all(spread(keys, values, queries, out_grad), "pipe", 0, 0, tiled=True)
    parts = parts.reshape(2 * WIDE, 4, HALF, HD)
    own = lax.all_to_all(parts, CHIPS, 0, 0, tiled=True)
    other = lax.ppermute(own[:, :2], "pipe", SWAP)
    first, mine, theirs = attend(place, picks, own, other)
    whole = combine(first, mine, lax.ppermute(theirs, "pipe", SWAP))

    back = lax.all_to_all(whole, CHIPS, 0, 0, tiled=True)
    got_out = lax.ppermute(back[:heads, 0], "pipe", [(0, 1)])
    got_grads = lax.ppermute(back[WIDE : WIDE + heads], "pipe", [(1, 0)])
    return tuple(gather(place, back, got_out, got_grads, heads))


def solution(mesh):
    placed = P("pipe", CHIPS, None)
    return jax.shard_map(
        on_device,
        mesh=mesh,
        in_specs=(placed,) * 4 + (P("pipe", None, None),),
        out_specs=(placed,) * 4,
        check_vma=False,
    )
```

time: 1040 us -> 215 us (0.21)
  waiting for transfers between devices: 413 us -> 9.32 us
  local copies, waits for them, and re-layouts: 244 us -> 6.21 us
  other arithmetic: 130 us -> 0.59 us
  matrix products: 116 us -> 0 us
  Pallas kernels: 0 us -> 72.4 us
  blocking collectives: 94 us -> 116 us
  between operations: 18.2 us -> 0.68 us
    reduce_scatter x1 -> x0, waiting for transfers between devices: 322 us -> none  [on_device(): lax.psum_scatter(padded[BLK:BLK + lax.axis_size('ctx') * rows], 'ctx', sc...]
    dot_general x49 -> x0, matrix products: 116 us -> none  [the longest x7 26 us: head_backward(): jnp.einsum('qk,qd->kd', low, grad, preferred_element_type=jnp.float32)]
    dynamic_update_slice x39 -> x0, local copies, waits for them, and re-layouts: 88.5 us -> none  [the longest x4 73.2 us: on_device(): padded = lax.dynamic_update_slice_in_dim(padded, current + piece, place, 0)]
    unnamed x5 -> x0, other arithmetic: 84.8 us -> none
    all_gather x2 -> x0, waiting for transfers between devices: 84.1 us -> none  [the longest x1 84.1 us: on_device(): lax.all_gather(v_heads, 'ctx', axis=1, tiled=True)]
    pallas_call x0 -> x4, Pallas kernels: none -> 72.4 us  [the longest x1 54.6 us: attend(): pl.pallas_call(attend_kernel, in_specs=[smem, smem, vmem, vmem], out_spec...]
    slice x2, local copies, waits for them, and re-layouts: 39.8 us -> 0.27 us  [the longest x1 0.17 us: on_device(): other = lax.ppermute(own[:, :2], 'pipe', SWAP)]
    unnamed x30 -> x12, local copies, waits for them, and re-layouts: 35.1 us -> 5.22 us
  transfers between devices with their start and end apart: 7 -> 5, of which waited for: 4 -> 3; matrix products, arithmetic and copies ran while one was open for 10% -> 1% of each run, Pallas kernels for 0% -> 0%
where the time goes in v1:
time: 215 us; the launch traced here: 214 us
  blocking collectives  116 us (54%)
  Pallas kernels  72.4 us (34%)
  waiting for transfers between devices  9.32 us (4%)
  starting transfers between devices  8.55 us (4%)
  local copies, waits for them, and re-layouts  6.21 us (3%)
    all_to_all x1, blocking collectives, on_device(): own = lax.all_to_all(parts, CHIPS, 0, 0, tiled=True)  61.7 us
    pallas_call x1, Pallas kernels, attend(): pl.pallas_call(attend_kernel, in_specs=[smem, smem, vmem, vmem], out_spec...  54.6 us
    all_to_all x1, blocking collectives, on_device(): back = lax.all_to_all(whole, CHIPS, 0, 0, tiled=True)  45.3 us
    all_to_all x1, blocking collectives, on_device(): lax.all_to_all(spread(keys, values, queries, out_grad), 'pipe', 0, 0, til...  9.53 us
    pallas_call x1, Pallas kernels, gather(): pl.pallas_call(gather_kernel, grid=(heads // STEP,), in_specs=[pl.BlockSp...  6.39 us
    pallas_call x1, Pallas kernels, spread(): pl.pallas_call(spread_kernel, grid=(heads // STEP,), in_specs=[item] * 4,...  6.32 us
    unnamed x12, local copies, waits for them, and re-layouts  5.22 us
    pallas_call x1, Pallas kernels, combine(): pl.pallas_call(combine_kernel, grid=(4,), in_specs=[pl.BlockSpec((size, H...  5.17 us
  transfers between devices with their start and end apart: 5, of which 3 were waited for; matrix products, arithmetic and copies ran while one was open for 1% of the time, Pallas kernels for 0%

profile of v1, /device:TPU:1, one launch (start us, length us, event | category | flops | bytes accessed | tf_op | source)
XLA Modules:
  0.0 214.3 jit_solution(16507358212056270824)
XLA Ops:
  0.6 6.3 %spread_heads.1 = bf16[2,32,4,64,128]{4,3,2,1,0:T(8,128)(2,1)} custom-call(bf16[1,128,3584]{2,1,0:T(8,128)(2,1)} %k_ref.1, bf16[1,128,3584]{2,1,0:T(8,128)(2,1)} %v_ref.1, bf16[1,128,3584]{2,1,0:T(8,128)(2,1)} %q_ref.1, bf16[1,128,3584]{2,1,0:T(8,128)(2,1)} %g_ref.1), custom_call_target="tpu_custom_call" | custom-call | tf_op jit(solution)/shard_map/spread_heads/pallas_call | solution.py:41
  6.9 9.5 %all_to_all.15 = bf16[2,32,4,64,128]{4,3,2,1,0:T(8,128)(2,1)S(1)} all-to-all(bf16[2,32,4,64,128]{4,3,2,1,0:T(8,128)(2,1)} %spread_heads.1), channel_id=1, replica_groups=mesh['pipe'=2,'ctx'=16,'tp'=4] {'pipe'}, dimensions={0} | all-to-all | bytes 8388608 | tf_op jit(solution)/shard_map/all_to_all | solution.py:237
  16.5 61.7 %all_to_all.16.own_ref = bf16[64,4,64,128]{3,2,1,0:T(8,128)(2,1)S(1)} all-to-all(bf16[64,4,64,128]{3,2,1,0:T(8,128)(2,1)S(1)} %bitcast.6), channel_id=1, replica_groups=mesh['pipe'=2,'ctx'=16,'tp'=4] {'ctx','tp'}, dimensions={0} | all-to-all | bytes 8388608 | tf_op jit(solution)/shard_map/all_to_all | solution.py:239
  78.1 0.0 copy-start.1
  78.1 2.0 copy-done.1
  80.1 0.0 copy-start.5
  80.1 0.2 slice.12
  80.3 2.4 %collective-permute-start.1 = (bf16[64,2,64,128]{3,2,1,0:T(8,128)(2,1)S(1)}, bf16[64,2,64,128]{3,2,1,0:T(8,128)(2,1)}, u32[]{:S(2)}, u32[]{:S(2)}) collective-permute-start(bf16[64,2,64,128]{3,2,1,0:T(8,128)(2,1)S(1)} %slice.12), channel_id=1, source_target_pairs={{0,64},{64,0},{1,65},{65,1},{2,66},{66,2},{3,67},{67,3},{4,68},{68... | collective-permute-start | bytes 6291464 | tf_op jit(solution)/shard_map/ppermute | solution.py:240
  82.7 0.0 copy-done.5
  82.7 0.4 collective-permute-start
  83.2 0.6 pad_add_fusion.place_ref
  83.7 2.8 %collective-permute-done = s32[1,16,3]{1,0,2:T(1,128)S(1)} collective-permute-done((s32[1,16,3]{1,0,2:T(1,128)S(1)}, s32[1,16,3]{1,0,2:T(1,128)S(1)}, u32[]{:S(2)}, u32[]{:S(2)}) %collective-permute-start) | collective-permute-done | bytes 224 | tf_op jit(solution)/shard_map/ppermute | solution.py:235
  86.5 0.7 copy.10
  87.2 0.0 collective-permute-done.1.other_ref
  87.2 54.6 %attend_head.1 = (bf16[64,64,128]{2,1,0:T(8,128)(2,1)}, f32[2,64,64,128]{3,2,1,0:T(8,128)}, bf16[2,64,64,128]{3,2,1,0:T(8,128)(2,1)}) custom-call(s32[2]{0:T(128)} %pad_add_fusion.place_ref, s32[16,3]{1,0:T(8,128)} %bitcast.7, bf16[64,4,64,128]{3,2,1,0:T(8,128)(2,1)} %copy-done.1, bf16[64,2,64,128]{3,2,1,0:T(8,128)(2,1)} %collective-permute-done.1.other_ref), custom_call_target="tpu_custom_call" | custom-call | flops 12884901888 | bytes 20971520 | tf_op jit(solution)/shard_map/attend_head/pallas_call | solution.py:145
  141.8 0.2 collective-permute-start.2
  142.0 4.1 %collective-permute-done.2.got_ref = bf16[2,64,64,128]{3,2,1,0:T(8,128)(2,1)S(1)} collective-permute-done((bf16[2,64,64,128]{3,2,1,0:T(8,128)(2,1)}, bf16[2,64,64,128]{3,2,1,0:T(8,128)(2,1)S(1)}, u32[]{:S(2)}, u32[]{:S(2)}) %collective-permute-start.2) | collective-permute-done | bytes 2097184 | tf_op jit(solution)/shard_map/ppermute | solution.py:242
  146.1 0.0 copy-start.2
  146.2 1.4 copy-done.2
  147.6 5.2 %combine_halves.1 = bf16[64,3,64,128]{3,2,1,0:T(8,128)(2,1)} custom-call(bf16[64,64,128]{2,1,0:T(8,128)(2,1)} %get-tuple-element.7.first_ref, f32[2,64,64,128]{3,2,1,0:T(8,128)} %get-tuple-element.8.mine_ref, bf16[2,64,64,128]{3,2,1,0:T(8,128)(2,1)} %copy-done.2), custom_call_target="tpu_custom_call" | custom-call | tf_op jit(solution)/shard_map/combine_halves/pallas_call | solution.py:176
  152.7 45.3 %all_to_all.17.ao_ref.ag_ref = bf16[64,3,64,128]{3,2,1,0:T(8,128)(2,1)S(1)} all-to-all(bf16[64,3,64,128]{3,2,1,0:T(8,128)(2,1)} %combine_halves.1), channel_id=1, replica_groups=mesh['pipe'=2,'ctx'=16,'tp'=4] {'ctx','tp'}, dimensions={0} | all-to-all | bytes 6291456 | tf_op jit(solution)/shard_map/all_to_all | solution.py:244
  198.0 0.0 copy-start
  198.0 0.1 slice.14
  198.1 4.1 %collective-permute-start.4 = (bf16[28,3,64,128]{3,2,1,0:T(8,128)(2,1)S(1)}, bf16[28,3,64,128]{3,2,1,0:T(8,128)(2,1)S(1)}, u32[]{:S(2)}, u32[]{:S(2)}) collective-permute-start(bf16[28,3,64,128]{3,2,1,0:T(8,128)(2,1)S(1)} %slice.14), channel_id=1, source_target_pairs={{64,0},{65,1},{66,2},{67,3},{68,4},{69,5},{70,6},{71,7},{72,8},{73... | collective-permute-start | bytes 4128776 | tf_op jit(solution)/shard_map/ppermute | solution.py:246
  202.3 1.3 collective-permute-start.3
  203.6 2.4 %collective-permute-done.3.bo_ref = bf16[28,64,128]{2,1,0:T(8,128)(2,1)S(1)} collective-permute-done((bf16[28,64,128]{2,1,0:T(8,128)(2,1)S(1)}, bf16[28,64,128]{2,1,0:T(8,128)(2,1)S(1)}, u32[]{:S(2)}, u32[]{:S(2)}) %collective-permute-start.3) | collective-permute-done | bytes 458784 | tf_op jit(solution)/shard_map/ppermute | solution.py:245
  206.0 0.0 copy-start.4
  206.0 0.0 collective-permute-done.4.bg_ref
  206.0 0.0 copy-done
  206.0 0.8 copy-done.4
  206.8 1.1 copy-done.3
  207.9 6.4 %gather_heads.1 = (bf16[1,128,3584]{2,1,0:T(8,128)(2,1)}, bf16[1,128,3584]{2,1,0:T(8,128)(2,1)}, bf16[1,128,3584]{2,1,0:T(8,128)(2,1)}, bf16[1,128,3584]{2,1,0:T(8,128)(2,1)}) custom-call(s32[2]{0:T(128)} %pad_add_fusion.place_ref, bf16[64,3,64,128]{3,2,1,0:T(8,128)(2,1)} %copy-done, bf16[64,3,64,128]{3,2,1,0:T(8,128)(2,1)} %copy-done, ...), custom_call_target="tpu_custom_call" | custom-call | tf_op jit(solution)/shard_map/gather_heads/pallas_call | solution.py:209
  (3 shorter events, 0.0 us)
Async XLA Ops:
  78.1 2.0 copy-start.1
  80.1 2.6 %copy-start.5 = (s32[1,16,3]{1,0,2:T(1,128)S(1)}, s32[1,16,3]{1,0,2:T(1,128)}, u32[]{:S(2)}) copy-start(s32[1,16,3]{1,0,2:T(1,128)} %param.9) | copy-start | bytes 580
  80.3 6.9 %collective-permute-start.1 = (bf16[64,2,64,128]{3,2,1,0:T(8,128)(2,1)S(1)}, bf16[64,2,64,128]{3,2,1,0:T(8,128)(2,1)}, u32[]{:S(2)}, u32[]{:S(2)}) collective-permute-start(bf16[64,2,64,128]{3,2,1,0:T(8,128)(2,1)S(1)} %slice.12), channel_id=1, source_target_pairs={{0,64},{64,0},{1,65},{65,1},{2,66},{66,2},{3,67},{67,3},{4,68},{68... | collective-permute-start | bytes 6291464 | tf_op jit(solution)/shard_map/ppermute | solution.py:240
  82.7 3.8 %collective-permute-start = (s32[1,16,3]{1,0,2:T(1,128)S(1)}, s32[1,16,3]{1,0,2:T(1,128)S(1)}, u32[]{:S(2)}, u32[]{:S(2)}) collective-permute-start(s32[1,16,3]{1,0,2:T(1,128)S(1)} %copy-done.5), channel_id=1, source_target_pairs={{0,64},{64,0},{1,65},{65,1},{2,66},{66,2},{3,67},{67,3},{4,68},{68... | collective-permute-start | bytes 584 | tf_op jit(solution)/shard_map/ppermute | solution.py:235
  141.8 4.4 %collective-permute-start.2 = (bf16[2,64,64,128]{3,2,1,0:T(8,128)(2,1)}, bf16[2,64,64,128]{3,2,1,0:T(8,128)(2,1)S(1)}, u32[]{:S(2)}, u32[]{:S(2)}) collective-permute-start(bf16[2,64,64,128]{3,2,1,0:T(8,128)(2,1)} %get-tuple-element.9), channel_id=1, source_target_pairs={{0,64},{64,0},{1,65},{65,1},{2,66},{66,2},{3,67},{67,3},{4,68},{68... | collective-permute-start | bytes 6291464 | tf_op jit(solution)/shard_map/ppermute | solution.py:242
  146.1 1.4 copy-start.2
  198.0 8.0 %copy-start = (bf16[64,3,64,128]{3,2,1,0:T(8,128)(2,1)}, bf16[64,3,64,128]{3,2,1,0:T(8,128)(2,1)S(1)}, u32[]{:S(2)}) copy-start(bf16[64,3,64,128]{3,2,1,0:T(8,128)(2,1)S(1)} %all_to_all.17.ao_ref.ag_ref) | copy-start | bytes 9437188
  198.1 7.9 %collective-permute-start.4 = (bf16[28,3,64,128]{3,2,1,0:T(8,128)(2,1)S(1)}, bf16[28,3,64,128]{3,2,1,0:T(8,128)(2,1)S(1)}, u32[]{:S(2)}, u32[]{:S(2)}) collective-permute-start(bf16[28,3,64,128]{3,2,1,0:T(8,128)(2,1)S(1)} %slice.14), channel_id=1, source_target_pairs={{64,0},{65,1},{66,2},{67,3},{68,4},{69,5},{70,6},{71,7},{72,8},{73... | collective-permute-start | bytes 4128776 | tf_op jit(solution)/shard_map/ppermute | solution.py:246
  202.3 3.7 %collective-permute-start.3 = (bf16[28,64,128]{2,1,0:T(8,128)(2,1)S(1)}, bf16[28,64,128]{2,1,0:T(8,128)(2,1)S(1)}, u32[]{:S(2)}, u32[]{:S(2)}) collective-permute-start(bf16[28,64,128]{2,1,0:T(8,128)(2,1)S(1)} %slice_bitcast_fusion), channel_id=1, source_target_pairs={{0,64},{1,65},{2,66},{3,67},{4,68},{5,69},{6,70},{7,71},{8,72},{9,... | collective-permute-start | bytes 1376264 | tf_op jit(solution)/shard_map/ppermute | solution.py:245
  206.0 0.8 copy-start.4
  206.8 1.1 copy-start.3

commit v2 on v1

v2 whole, which is shorter than its diff:
```python
import math

import jax
import jax.numpy as jnp
from jax import lax
from jax.experimental import pallas as pl
from jax.experimental.pallas import tpu as pltpu
from jax.sharding import PartitionSpec as P

HD = 128
BLK = 512
TOPK = 3
HALF = 64
PART = 4
ROWS = PART * HALF
KEYS = 2 * (TOPK + 1) * ROWS
WIDE = 32
GROUP = 7
MIB = 1024 * 1024

BF = jnp.bfloat16
F32 = jnp.float32
NN = ((1,), (0,))
SMEM = pl.BlockSpec(memory_space=pltpu.SMEM)
ANY = pl.BlockSpec(memory_space=pl.ANY)


def dot(a, b):
    return lax.dot_general(a, b, (NN, ((), ())), preferred_element_type=F32)


def call(kernel, name, out_shape, n_smem, n_any, scratch, vmem, moved, flops=0, aliases=None):
    one = not isinstance(out_shape, list)
    return pl.pallas_call(
        kernel,
        in_specs=[SMEM] * n_smem + [ANY] * n_any,
        out_specs=ANY if one else [ANY] * len(out_shape),
        out_shape=out_shape,
        scratch_shapes=scratch,
        input_output_aliases=aliases or {},
        compiler_params=pltpu.CompilerParams(vmem_limit_bytes=vmem * MIB),
        cost_estimate=pl.CostEstimate(flops=flops, bytes_accessed=moved, transcendentals=0),
        name=name,
    )


def spread(core, arrays, base, whole=None):
    heads = arrays[0].shape[-1] // HD
    groups = heads // GROUP

    def kernel(place_ref, *refs):
        sources = refs[:4] if len(arrays) == 4 else [refs[0].at[a] for a in range(4)]
        out_ref, got, cut, in_sem, out_sem = refs[-5:]

        def load(g, a):
            return pltpu.make_async_copy(
                sources[a].at[0:HALF, pl.ds(g * GROUP * HD, GROUP * HD)], got.at[g, a], in_sem.at[g, a]
            )

        def store(g):
            at = pl.ds(place_ref[0] * WIDE + g * GROUP, GROUP)
            return pltpu.make_async_copy(cut.at[pl.ds(g * GROUP, GROUP)], out_ref.at[at], out_sem.at[g])

        for g in range(groups):
            for a in range(4):
                load(g, a).start()
        for g in range(groups):
            for a in range(4):
                load(g, a).wait()
                for h in range(GROUP):
                    cut[g * GROUP + h, a] = got[g, a, :, h * HD : (h + 1) * HD]
            store(g).start()
        for g in range(groups):
            store(g).wait()

    extra = [] if whole is None else [whole]
    return call(
        kernel, "spread_heads",
        jax.ShapeDtypeStruct((2 * WIDE, 4, HALF, HD), BF), 1, len(arrays) + len(extra),
        [
            pltpu.VMEM((groups, 4, HALF, GROUP * HD), BF),
            pltpu.VMEM((heads, 4, HALF, HD), BF),
            pltpu.SemaphoreType.DMA((groups, 4)),
            pltpu.SemaphoreType.DMA((groups,)),
        ],
        50 if extra else 56, 4 << 20, aliases={1 + len(arrays): 0} if extra else None,
    )(base[None], *arrays, *extra)


def attend_kernel(
    place_ref, picks_ref, own_hbm, other_hbm,
    first_hbm, mine_hbm, theirs_hbm,
    own_ref, other_ref, kt_ref, vt_ref, s0_ref, s1_ref, t0_ref, t1_ref, low_ref, ds_ref,
    mine_ref, sum_ref, theirs_ref, first_ref, in_sem, first_sem, mine_sem, theirs_sem,
):
    nb = picks_ref.shape[0]
    half_at, seg = place_ref[0], place_ref[1]
    scale = 1.0 / math.sqrt(HD)
    power = scale * math.log2(math.e)
    s_refs, t_refs = (s0_ref, s1_ref), (t0_ref, t1_ref)
    chunks = [(j, half) for j in range(TOPK + 1) for half in range(2)]
    rows = [pl.ds(n * ROWS, ROWS) for n in range(len(chunks))]

    def loads(b):
        at = pl.ds(b * PART, PART)
        return (
            pltpu.make_async_copy(own_hbm.at[at], own_ref.at[at], in_sem.at[b, 0]),
            pltpu.make_async_copy(other_hbm.at[at], other_ref.at[at], in_sem.at[b, 1]),
        )

    def start(b, carry):
        for copy in loads(b):
            copy.start()
        return carry

    def arrive(b):
        for copy in loads(b):
            copy.wait()

    def part(a, half, b):
        ref = own_ref if half == 0 else other_ref
        return ref[pl.ds(b * PART, PART), a].reshape(ROWS, HD)

    def slots_of(i):
        return [picks_ref[i, j] for j in range(TOPK)] + [i]

    def turn(b):
        for half in range(2):
            kt_ref[half * nb + b] = part(0, half, b).T
            vt_ref[half * nb + b] = part(1, half, b).T

    def scores(i, buf):
        qt = part(2, 0, i).T
        slots = slots_of(i)
        key_at = lax.broadcasted_iota(jnp.int32, (ROWS, ROWS), 0)
        query_at = lax.broadcasted_iota(jnp.int32, (ROWS, ROWS), 1)
        top = jnp.full((1, ROWS), -jnp.inf, F32)
        for n, (j, half) in enumerate(chunks):
            s = dot(part(0, half, slots[j]), qt)
            if j < TOPK:
                valid = slots[j] < i
            elif half == 0:
                valid = key_at <= query_at
            else:
                valid = key_at // HALF < query_at // HALF + half_at
            s = jnp.where(valid, s, -jnp.inf)
            s_refs[buf][rows[n]] = s
            top = jnp.maximum(top, jnp.max(s, axis=0, keepdims=True))
        t_refs[buf][...] = jnp.broadcast_to(top, (8, ROWS))

    def add_terms(a, terms, slots):
        for n, (j, half) in enumerate(chunks):
            acc = mine_ref if half == 0 else sum_ref
            at = pl.ds(slots[j] * PART, PART)
            term = terms[n * ROWS : (n + 1) * ROWS].reshape(PART, HALF, HD)
            if j < TOPK:
                acc[a, at] += term
            else:
                acc[a, at] = term

    def flat(ref, slots):
        return jnp.concatenate([ref[half * nb + slots[j]] for j, half in chunks], axis=1)

    def rest(i, buf):
        s_ref = s_refs[buf]
        q, g = part(2, 0, i), part(3, 0, i)
        gt = g.T
        slots = slots_of(i)
        top = t_refs[buf][0:1]
        total = jnp.zeros((1, ROWS), F32)
        for n in range(len(chunks)):
            e = jnp.exp2((s_ref[rows[n]] - top) * power)
            s_ref[rows[n]] = e
            total = total + jnp.sum(e, axis=0, keepdims=True)
        inverse = 1.0 / total
        for n in range(len(chunks)):
            low_ref[rows[n]] = (s_ref[rows[n]] * inverse).astype(BF)
        out_t = dot(flat(vt_ref, slots), low_ref[...])
        add_terms(1, dot(low_ref[...], g), slots)
        out = out_t.T.astype(BF)
        delta = jnp.sum(gt.astype(F32) * out_t.astype(BF).astype(F32), axis=0, keepdims=True)
        for n, (j, half) in enumerate(chunks):
            dp = dot(part(1, half, slots[j]), gt)
            ds_ref[rows[n]] = (s_ref[rows[n]] * inverse * (dp - delta)).astype(BF)
        query_t = dot(flat(kt_ref, slots), ds_ref[...])
        add_terms(0, dot(ds_ref[...], q), slots)
        query = (query_t * scale).T.astype(BF)
        first = jnp.where(seg == 0, out.astype(F32), query.astype(F32)).astype(BF)
        first_ref[pl.ds(i * PART, PART)] = first.reshape(PART, HALF, HD)

    def send_first(p):
        at = pl.ds(p * 2 * PART, 2 * PART)
        return pltpu.make_async_copy(first_ref.at[at], first_hbm.at[at, 0], first_sem.at[p])

    lax.fori_loop(0, nb, start, 0)
    arrive(0)
    turn(0)
    scores(0, 0)

    def pair(p, carry):
        i = 2 * p
        later = jnp.minimum(i + 2, nb - 1)
        arrive(i + 1)

        @pl.when(i + 2 < nb)
        def _():
            arrive(i + 2)

        turn(i + 1)
        turn(later)
        scores(i + 1, 1)
        rest(i, 0)
        scores(later, 0)
        rest(i + 1, 1)
        send_first(p).start()
        return carry

    lax.fori_loop(0, nb // 2, pair, 0)

    def send_mine(a):
        return pltpu.make_async_copy(mine_ref.at[a], mine_hbm.at[a], mine_sem.at[a])

    def send_theirs(b):
        at = pl.ds(b * 4 * PART, 4 * PART)
        return pltpu.make_async_copy(theirs_ref.at[:, at], theirs_hbm.at[:, at], theirs_sem.at[b])

    for a in range(2):
        send_mine(a).start()
    for b in range(nb // 4):
        at = pl.ds(b * 4 * PART, 4 * PART)
        for a in range(2):
            theirs_ref[a, at] = sum_ref[a, at].astype(BF)
        send_theirs(b).start()
    for p in range(nb // 2):
        send_first(p).wait()
    for a in range(2):
        send_mine(a).wait()
    for b in range(nb // 4):
        send_theirs(b).wait()


def attend(place, picks, own, other):
    nb = picks.shape[0]
    n = nb * PART
    work = 6 * 2 * nb * ROWS * KEYS * HD
    return call(
        attend_kernel, "attend_head",
        [
            jax.ShapeDtypeStruct((n, 3, HALF, HD), BF),
            jax.ShapeDtypeStruct((2, n, HALF, HD), F32),
            jax.ShapeDtypeStruct((2, n, HALF, HD), BF),
        ],
        2, 2,
        [
            pltpu.VMEM((n, 4, HALF, HD), BF),
            pltpu.VMEM((n, 2, HALF, HD), BF),
            pltpu.VMEM((2 * nb, HD, ROWS), BF),
            pltpu.VMEM((2 * nb, HD, ROWS), BF),
            pltpu.VMEM((KEYS, ROWS), F32),
            pltpu.VMEM((KEYS, ROWS), F32),
            pltpu.VMEM((8, ROWS), F32),
            pltpu.VMEM((8, ROWS), F32),
            pltpu.VMEM((KEYS, ROWS), BF),
            pltpu.VMEM((KEYS, ROWS), BF),
            pltpu.VMEM((2, n, HALF, HD), F32),
            pltpu.VMEM((2, n, HALF, HD), F32),
            pltpu.VMEM((2, n, HALF, HD), BF),
            pltpu.VMEM((n, HALF, HD), BF),
            pltpu.SemaphoreType.DMA((nb, 2)),
            pltpu.SemaphoreType.DMA((nb // 2,)),
            pltpu.SemaphoreType.DMA((2,)),
            pltpu.SemaphoreType.DMA((nb // 4,)),
        ],
        42, 16 << 20, work,
    )(place, picks, own, other)


def combine(whole, mine, got):
    n = whole.shape[0]
    groups = 4
    size = n // groups

    def kernel(whole_ref, mine_hbm, got_hbm, out_hbm, mine_ref, got_ref, out_ref, in_sem, out_sem):
        scale = 1.0 / math.sqrt(HD)
        at = [pl.ds(g * size, size) for g in range(groups)]

        def loads(g):
            return (
                pltpu.make_async_copy(mine_hbm.at[:, at[g]], mine_ref.at[:, at[g]], in_sem.at[g, 0]),
                pltpu.make_async_copy(got_hbm.at[:, at[g]], got_ref.at[:, at[g]], in_sem.at[g, 1]),
            )

        def store(g):
            return pltpu.make_async_copy(out_ref.at[at[g]], out_hbm.at[at[g], 1:3], out_sem.at[g])

        for g in range(groups):
            for copy in loads(g):
                copy.start()
        for g in range(groups):
            for copy in loads(g):
                copy.wait()
            for a in range(2):
                value = mine_ref[a, at[g]] + got_ref[a, at[g]].astype(F32)
                out_ref[at[g], a] = (value * scale if a == 0 else value).astype(BF)
            store(g).start()
        for g in range(groups):
            store(g).wait()

    return call(
        kernel, "combine_halves", jax.ShapeDtypeStruct(whole.shape, BF), 0, 3,
        [
            pltpu.VMEM((2, n, HALF, HD), F32),
            pltpu.VMEM((2, n, HALF, HD), BF),
            pltpu.VMEM((n, 2, HALF, HD), BF),
            pltpu.SemaphoreType.DMA((groups, 2)),
            pltpu.SemaphoreType.DMA((groups,)),
        ],
        12, 8 << 20, aliases={0: 0},
    )(whole, mine, got)


def gather(core, source, base, high, results=None):
    heads = 4 * GROUP
    groups = heads // GROUP
    rows = slice(HALF, 2 * HALF) if high else slice(0, HALF)

    def kernel(place_ref, source_ref, *refs):
        outs = refs[-8:-4]
        got, cut, in_sem, out_sem = refs[-4:]

        def load(g):
            at = pl.ds(place_ref[1] + g * GROUP, GROUP)
            return pltpu.make_async_copy(source_ref.at[at], got.at[g], in_sem.at[g])

        def store(g, a):
            cols = pl.ds(g * GROUP * HD, GROUP * HD)
            return pltpu.make_async_copy(cut.at[g, a], outs[a].at[0, rows, cols], out_sem.at[g, a])

        for g in range(groups):
            load(g).start()
        for g in range(groups):
            load(g).wait()
            for a in range(4):
                live = place_ref[0] == (1 if a == 0 else 0)
                for h in range(GROUP):
                    value = got[g, h, max(a - 1, 0)]
                    cut[g, a, :, h * HD : (h + 1) * HD] = jnp.where(live, value, jnp.zeros_like(value))
                store(g, a).start()
        for g in range(groups):
            for a in range(4):
                store(g, a).wait()

    extra = [] if results is None else list(results)
    return call(
        kernel, "gather_heads", [jax.ShapeDtypeStruct((1, 2 * HALF, heads * HD), BF)] * 4, 1, 1 + len(extra),
        [
            pltpu.VMEM((groups, GROUP, 3, HALF, HD), BF),
            pltpu.VMEM((groups, 4, HALF, GROUP * HD), BF),
            pltpu.SemaphoreType.DMA((groups,)),
            pltpu.SemaphoreType.DMA((groups, 4)),
        ],
        8, 4 << 20, aliases={2 + a: a for a in range(4)} if extra else None,
    )(jnp.stack([core, base]), source, *extra)


def cut_out(name, out_shape, vmem, pieces, place, *sources):
    def kernel(place_ref, *refs):
        out_ref, held, in_sem, out_sem = refs[-4:]
        copies = []
        for n, (src, at) in enumerate(pieces(place_ref, refs[:-4])):
            there = pltpu.make_async_copy(src, held.at[at], in_sem.at[n])
            copies.append((there, pltpu.make_async_copy(held.at[at], out_ref.at[at], out_sem.at[n])))
        for there, _ in copies:
            there.start()
        for there, back in copies:
            there.wait()
            back.start()
        for _, back in copies:
            back.wait()

    return call(
        kernel, name, jax.ShapeDtypeStruct(out_shape, BF), 1, len(sources),
        [pltpu.VMEM(out_shape, BF), pltpu.SemaphoreType.DMA((4,)), pltpu.SemaphoreType.DMA((4,))],
        vmem, 2 << 20,
    )(place[None], *sources)


CHIPS = ("ctx", "tp")
SWAP = [(0, 1), (1, 0)]


def on_device(queries, keys, values, out_grad, chosen):
    heads = queries.shape[2] // HD
    core = lax.axis_index("pipe").astype(jnp.int32)
    seg = (lax.axis_index(CHIPS) // WIDE).astype(jnp.int32)

    place = jnp.stack([core ^ seg, seg])
    arrays = (keys, values, queries, out_grad)
    theirs = cut_out(
        "cut_tokens", (4, HALF, heads * HD), 56,
        lambda _, refs: [(ref.at[0, HALF : 2 * HALF], a) for a, ref in enumerate(refs)],
        core, *arrays,
    )
    got = lax.ppermute(theirs, "pipe", SWAP)
    other_chosen = lax.ppermute(chosen, "pipe", SWAP)
    parts = spread(core, [x[0] for x in arrays], core)
    parts = spread(core, [got], 1 - core, parts)
    picks = jnp.where(seg == core, chosen, other_chosen)[0]
    parts, picks, place = lax.optimization_barrier((parts, picks, place))

    own = lax.all_to_all(parts, CHIPS, 0, 0, tiled=True)
    n = own.shape[0]
    mine = cut_out(
        "cut_keys", (n, 2, HALF, HD), 56,
        lambda _, refs: [
            (refs[0].at[pl.ds(g * n // 4, n // 4), 0:2], pl.ds(g * n // 4, n // 4)) for g in range(4)
        ],
        core, own,
    )
    other = lax.ppermute(mine, "pipe", SWAP)
    first, mine, theirs = attend(place, picks, own, other)
    whole = combine(first, mine, lax.ppermute(theirs, "pipe", SWAP))

    back = lax.all_to_all(whole, CHIPS, 0, 0, tiled=True)
    theirs = cut_out(
        "cut_heads", (heads, 3, HALF, HD), 4,
        lambda place_ref, refs: [
            (refs[0].at[pl.ds(place_ref[0] * WIDE + g * GROUP, GROUP)], pl.ds(g * GROUP, GROUP)) for g in range(4)
        ],
        core, back,
    )
    got = lax.ppermute(theirs, "pipe", SWAP)
    results = gather(core, back, (1 - core) * WIDE, True)
    return tuple(gather(core, got, core * 0, False, results))


def solution(mesh):
    placed = P("pipe", CHIPS, None)
    return jax.shard_map(
        on_device,
        mesh=mesh,
        in_specs=(placed,) * 4 + (P("pipe", None, None),),
        out_specs=(placed,) * 4,
        check_vma=False,
    )
```

time: 215 us -> 176 us (0.82)
  Pallas kernels: 72.4 us -> 51.1 us
  blocking collectives: 116 us -> 107 us
  local copies, waits for them, and re-layouts: 6.21 us -> 0.09 us
    pallas_call x4 -> x9, Pallas kernels: 72.4 us -> 51.1 us  [the longest x1 33.8 us: attend(): call(attend_kernel, 'attend_head', [jax.ShapeDtypeStruct((n, 3, HALF, HD)...]
    all_to_all x1 -> x0, blocking collectives: 9.53 us -> none  [on_device(): lax.all_to_all(spread(keys, values, queries, out_grad), 'pipe', 0, 0, til...]
    unnamed x12 -> x3, local copies, waits for them, and re-layouts: 5.22 us -> 0.01 us
  transfers between devices with their start and end apart: 5 -> 5, of which waited for: 3 -> 5; matrix products, arithmetic and copies ran while one was open for 1% -> 0% of each run, Pallas kernels for 0% -> 3%
where the time goes in v2:
time: 176 us; the launch traced here: 175 us
  blocking collectives  107 us (61%)
  Pallas kernels  51.1 us (29%)
  waiting for transfers between devices  9.09 us (5%)
  starting transfers between devices  6.71 us (4%)
    all_to_all x1, blocking collectives, on_device(): own = lax.all_to_all(parts, CHIPS, 0, 0, tiled=True)  62 us
    all_to_all x1, blocking collectives, on_device(): back = lax.all_to_all(whole, CHIPS, 0, 0, tiled=True)  45.2 us
    pallas_call x1, Pallas kernels, attend(): call(attend_kernel, 'attend_head', [jax.ShapeDtypeStruct((n, 3, HALF, HD)...  33.8 us
    pallas_call x3, Pallas kernels, cut_out(): call(kernel, name, jax.ShapeDtypeStruct(out_shape, BF), 1, len(sources),...  6.44 us
    pallas_call x2, Pallas kernels, gather(): call(kernel, 'gather_heads', [jax.ShapeDtypeStruct((1, 2 * HALF, heads *...  5.39 us
    pallas_call x2, Pallas kernels, spread(): call(kernel, 'spread_heads', jax.ShapeDtypeStruct((2 * WIDE, 4, HALF, HD)...  4.31 us
    ppermute x1, waiting for transfers between devices, on_device(): other = lax.ppermute(mine, 'pipe', SWAP)  3.91 us
    ppermute x1, waiting for transfers between devices, on_device(): whole = combine(first, mine, lax.ppermute(theirs, 'pipe', SWAP))  3.79 us
  transfers between devices with their start and end apart: 5, of which 5 were waited for; matrix products, arithmetic and copies ran while one was open for 0% of the time, Pallas kernels for 3%

profile of v2, /device:TPU:1, one launch (start us, length us, event | category | flops | bytes accessed | tf_op | source)
XLA Modules:
  0.0 175.2 jit_solution(17716572817832355789)
XLA Ops:
  0.6 0.0 copy-start
  0.6 2.3 %cut_tokens.1 = bf16[4,64,3584]{2,1,0:T(8,128)(2,1)} custom-call(s32[1]{0:T(128)} %bitcast.place_ref, bf16[1,128,3584]{2,1,0:T(8,128)(2,1)} %refs_0_.1, bf16[1,128,3584]{2,1,0:T(8,128)(2,1)} %refs_1_.1, bf16[1,128,3584]{2,1,0:T(8,128)(2,1)} %refs_2_.1, bf16[1,128,3584]{2,1,0:T(8,128)(2,1)} %refs_3_.1), custom_call_target="tpu_custom_call" | custom-call | bytes 2097152 | tf_op jit(solution)/shard_map/cut_tokens/pallas_call | solution.py:381
  3.0 1.5 collective-permute-start
  4.5 0.0 copy-done
  4.5 0.1 collective-permute-start.1
  4.6 0.1 pad_add_fusion.1.place_ref
  4.7 2.5 %spread_heads.2.refs_1_ = bf16[64,4,64,128]{3,2,1,0:T(8,128)(2,1)} custom-call(s32[1]{0:T(128)} %bitcast.place_ref, bf16[128,3584]{1,0:T(8,128)(2,1)} %bitcast.12, bf16[128,3584]{1,0:T(8,128)(2,1)} %bitcast.13, bf16[128,3584]{1,0:T(8,128)(2,1)} %bitcast.14, bf16[128,3584]{1,0:T(8,128)(2,1)} %bitcast.15), custom_call_target="tpu_custom_call" | custom-call | bytes 4194304 | tf_op jit(solution)/shard_map/spread_heads/pallas_call | solution.py:77
  7.2 0.6 collective-permute-done.1
  7.8 0.3 collective-permute-done.refs_0_
  8.1 1.8 %spread_heads.3 = bf16[64,4,64,128]{3,2,1,0:T(8,128)(2,1)} custom-call(s32[1]{0:T(128)} %bitcast.1.place_ref, bf16[4,64,3584]{2,1,0:T(8,128)(2,1)S(1)} %collective-permute-done.refs_0_, bf16[64,4,64,128]{3,2,1,0:T(8,128)(2,1)} %spread_heads.2.refs_1_), custom_call_target="tpu_custom_call", output_to_operand_aliasing={{}: (2, {})} | custom-call | bytes 4194304 | tf_op jit(solution)/shard_map/spread_heads/pallas_call | solution.py:77
  9.9 62.0 %all_to_all.10.refs_0_.own_hbm = bf16[64,4,64,128]{3,2,1,0:T(8,128)(2,1)} all-to-all(bf16[64,4,64,128]{3,2,1,0:T(8,128)(2,1)} %spread_heads.3), channel_id=1, replica_groups=mesh['pipe'=2,'ctx'=16,'tp'=4] {'ctx','tp'}, dimensions={0} | all-to-all | bytes 8388608 | tf_op jit(solution)/shard_map/all_to_all | solution.py:411
  71.9 2.4 %cut_keys.1 = bf16[64,2,64,128]{3,2,1,0:T(8,128)(2,1)} custom-call(s32[1]{0:T(128)} %bitcast.place_ref, bf16[64,4,64,128]{3,2,1,0:T(8,128)(2,1)} %all_to_all.10.refs_0_.own_hbm), custom_call_target="tpu_custom_call" | custom-call | bytes 2097152 | tf_op jit(solution)/shard_map/cut_keys/pallas_call | solution.py:381
  74.4 2.4 %collective-permute-start.2 = (bf16[64,2,64,128]{3,2,1,0:T(8,128)(2,1)}, bf16[64,2,64,128]{3,2,1,0:T(8,128)(2,1)S(1)}, u32[]{:S(2)}, u32[]{:S(2)}) collective-permute-start(bf16[64,2,64,128]{3,2,1,0:T(8,128)(2,1)} %cut_keys.1), channel_id=1, source_target_pairs={{0,64},{64,0},{1,65},{65,1},{2,66},{66,2},{3,67},{67,3},{4,68},{68... | collective-permute-start | bytes 6291464 | tf_op jit(solution)/shard_map/ppermute | solution.py:420
  76.8 0.1 copy.15.picks_ref
  76.9 3.9 %collective-permute-done.2.other_hbm = bf16[64,2,64,128]{3,2,1,0:T(8,128)(2,1)S(1)} collective-permute-done((bf16[64,2,64,128]{3,2,1,0:T(8,128)(2,1)}, bf16[64,2,64,128]{3,2,1,0:T(8,128)(2,1)S(1)}, u32[]{:S(2)}, u32[]{:S(2)}) %collective-permute-start.2) | collective-permute-done | bytes 2097184 | tf_op jit(solution)/shard_map/ppermute | solution.py:420
  80.8 33.8 %attend_head.1 = (bf16[64,3,64,128]{3,2,1,0:T(8,128)(2,1)S(1)}, f32[2,64,64,128]{3,2,1,0:T(8,128)S(1)}, bf16[2,64,64,128]{3,2,1,0:T(8,128)(2,1)S(1)}) custom-call(s32[2]{0:T(128)S(1)} %pad_add_fusion.1.place_ref, s32[16,3]{1,0:T(8,128)S(1)} %copy.15.picks_ref, bf16[64,4,64,128]{3,2,1,0:T(8,128)(2,1)} %all_to_all.10.refs_0_.own_hbm, ...), custom_call_target="tpu_custom_call" | custom-call | flops 12884901888 | bytes 16777216 | tf_op jit(solution)/shard_map/attend_head/pallas_call | solution.py:246
  114.7 0.5 collective-permute-start.3
  115.1 3.8 %collective-permute-done.3.got_hbm = bf16[2,64,64,128]{3,2,1,0:T(8,128)(2,1)S(1)} collective-permute-done((bf16[2,64,64,128]{3,2,1,0:T(8,128)(2,1)S(1)}, bf16[2,64,64,128]{3,2,1,0:T(8,128)(2,1)S(1)}, u32[]{:S(2)}, u32[]{:S(2)}) %collective-permute-start.3) | collective-permute-done | bytes 2097184 | tf_op jit(solution)/shard_map/ppermute | solution.py:422
  118.9 1.1 combine_halves.1
  120.0 45.2 %all_to_all.11.refs_0_.source_ref = bf16[64,3,64,128]{3,2,1,0:T(8,128)(2,1)S(1)} all-to-all(bf16[64,3,64,128]{3,2,1,0:T(8,128)(2,1)S(1)} %combine_halves.1), channel_id=1, replica_groups=mesh['pipe'=2,'ctx'=16,'tp'=4] {'ctx','tp'}, dimensions={0} | all-to-all | bytes 6291456 | tf_op jit(solution)/shard_map/all_to_all | solution.py:424
  165.2 1.7 cut_heads.1
  166.9 2.2 %collective-permute-start.4 = (bf16[28,3,64,128]{3,2,1,0:T(8,128)(2,1)}, bf16[28,3,64,128]{3,2,1,0:T(8,128)(2,1)}, u32[]{:S(2)}, u32[]{:S(2)}) collective-permute-start(bf16[28,3,64,128]{3,2,1,0:T(8,128)(2,1)} %cut_heads.1), channel_id=1, source_target_pairs={{0,64},{64,0},{1,65},{65,1},{2,66},{66,2},{3,67},{67,3},{4,68},{68... | collective-permute-start | bytes 4128776 | tf_op jit(solution)/shard_map/ppermute | solution.py:432
  169.2 0.1 pad_add_fusion.2.place_ref
  169.2 0.1 pad_add_fusion.place_ref
  169.3 2.5 %gather_heads.2 = (bf16[1,128,3584]{2,1,0:T(8,128)(2,1)}, bf16[1,128,3584]{2,1,0:T(8,128)(2,1)}, bf16[1,128,3584]{2,1,0:T(8,128)(2,1)}, bf16[1,128,3584]{2,1,0:T(8,128)(2,1)}) custom-call(s32[2]{0:T(128)S(1)} %pad_add_fusion.2.place_ref, bf16[64,3,64,128]{3,2,1,0:T(8,128)(2,1)S(1)} %all_to_all.11.refs_0_.source_ref), custom_call_target="tpu_custom_call" | custom-call | bytes 4194304 | tf_op jit(solution)/shard_map/gather_heads/pallas_call | solution.py:354
  171.8 0.5 collective-permute-done.4.source_ref
  172.3 2.9 %gather_heads.3 = (bf16[1,128,3584]{2,1,0:T(8,128)(2,1)}, bf16[1,128,3584]{2,1,0:T(8,128)(2,1)}, bf16[1,128,3584]{2,1,0:T(8,128)(2,1)}, bf16[1,128,3584]{2,1,0:T(8,128)(2,1)}) custom-call(s32[2]{0:T(128)S(1)} %pad_add_fusion.place_ref, ...), custom_call_target="tpu_custom_call", output_to_operand_aliasing={{0}: (2, {}), {1}: (3, {}), {2}: (4, {}), {3}: (5, {})} | custom-call | bytes 4194304 | tf_op jit(solution)/shard_map/gather_heads/pallas_call | solution.py:354
  (2 shorter events, 0.0 us)
Async XLA Ops:
  0.6 3.9 %copy-start = (s32[1,16,3]{1,0,2:T(1,128)S(1)}, s32[1,16,3]{1,0,2:T(1,128)}, u32[]{:S(2)}) copy-start(s32[1,16,3]{1,0,2:T(1,128)} %param.9) | copy-start | bytes 580
  3.0 5.1 %collective-permute-start = (bf16[4,64,3584]{2,1,0:T(8,128)(2,1)}, bf16[4,64,3584]{2,1,0:T(8,128)(2,1)S(1)}, u32[]{:S(2)}, u32[]{:S(2)}) collective-permute-start(bf16[4,64,3584]{2,1,0:T(8,128)(2,1)} %cut_tokens.1), channel_id=1, source_target_pairs={{0,64},{64,0},{1,65},{65,1},{2,66},{66,2},{3,67},{67,3},{4,68},{68... | collective-permute-start | bytes 5505032 | tf_op jit(solution)/shard_map/ppermute | solution.py:404
  4.5 3.3 %collective-permute-start.1 = (s32[1,16,3]{1,0,2:T(1,128)S(1)}, s32[1,16,3]{1,0,2:T(1,128)S(1)}, u32[]{:S(2)}, u32[]{:S(2)}) collective-permute-start(s32[1,16,3]{1,0,2:T(1,128)S(1)} %copy-done), channel_id=1, source_target_pairs={{0,64},{64,0},{1,65},{65,1},{2,66},{66,2},{3,67},{67,3},{4,68},{68... | collective-permute-start | bytes 584 | tf_op jit(solution)/shard_map/ppermute | solution.py:405
  74.4 6.4 %collective-permute-start.2 = (bf16[64,2,64,128]{3,2,1,0:T(8,128)(2,1)}, bf16[64,2,64,128]{3,2,1,0:T(8,128)(2,1)S(1)}, u32[]{:S(2)}, u32[]{:S(2)}) collective-permute-start(bf16[64,2,64,128]{3,2,1,0:T(8,128)(2,1)} %cut_keys.1), channel_id=1, source_target_pairs={{0,64},{64,0},{1,65},{65,1},{2,66},{66,2},{3,67},{67,3},{4,68},{68... | collective-permute-start | bytes 6291464 | tf_op jit(solution)/shard_map/ppermute | solution.py:420
  114.7 4.2 %collective-permute-start.3 = (bf16[2,64,64,128]{3,2,1,0:T(8,128)(2,1)S(1)}, bf16[2,64,64,128]{3,2,1,0:T(8,128)(2,1)S(1)}, u32[]{:S(2)}, u32[]{:S(2)}) collective-permute-start(bf16[2,64,64,128]{3,2,1,0:T(8,128)(2,1)S(1)} %get-tuple-element.19), channel_id=1, source_target_pairs={{0,64},{64,0},{1,65},{65,1},{2,66},{66,2},{3,67},{67,3},{4,68},{68... | collective-permute-start | bytes 6291464 | tf_op jit(solution)/shard_map/ppermute | solution.py:422
  166.9 5.3 %collective-permute-start.4 = (bf16[28,3,64,128]{3,2,1,0:T(8,128)(2,1)}, bf16[28,3,64,128]{3,2,1,0:T(8,128)(2,1)}, u32[]{:S(2)}, u32[]{:S(2)}) collective-permute-start(bf16[28,3,64,128]{3,2,1,0:T(8,128)(2,1)} %cut_heads.1), channel_id=1, source_target_pairs={{0,64},{64,0},{1,65},{65,1},{2,66},{66,2},{3,67},{67,3},{4,68},{68... | collective-permute-start | bytes 4128776 | tf_op jit(solution)/shard_map/ppermute | solution.py:432

commit v3 on v2

--- a/solution.py
+++ b/solution.py
@@ -90,7 +90,7 @@
 def attend_kernel(
     place_ref, picks_ref, own_hbm, other_hbm,
     first_hbm, mine_hbm, theirs_hbm,
-    own_ref, other_ref, kt_ref, vt_ref, s0_ref, s1_ref, t0_ref, t1_ref, low_ref, ds_ref,
+    own_ref, other_ref, kt_ref, vt_ref, s0_ref, s1_ref, t0_ref, t1_ref, d_ref, low_ref, ds_ref,
     mine_ref, sum_ref, theirs_ref, first_ref, in_sem, first_sem, mine_sem, theirs_sem,
 ):
     nb = picks_ref.shape[0]
@@ -134,7 +134,7 @@
         slots = slots_of(i)
         key_at = lax.broadcasted_iota(jnp.int32, (ROWS, ROWS), 0)
         query_at = lax.broadcasted_iota(jnp.int32, (ROWS, ROWS), 1)
-        top = jnp.full((1, ROWS), -jnp.inf, F32)
+        top = jnp.full((8, ROWS), -jnp.inf, F32)
         for n, (j, half) in enumerate(chunks):
             s = dot(part(0, half, slots[j]), qt)
             if j < TOPK:
@@ -145,8 +145,8 @@
                 valid = key_at // HALF < query_at // HALF + half_at
             s = jnp.where(valid, s, -jnp.inf)
             s_refs[buf][rows[n]] = s
-            top = jnp.maximum(top, jnp.max(s, axis=0, keepdims=True))
-        t_refs[buf][...] = jnp.broadcast_to(top, (8, ROWS))
+            top = jnp.maximum(top, jnp.max(s.reshape(ROWS // 8, 8, ROWS), axis=0))
+        t_refs[buf][...] = jnp.broadcast_to(jnp.max(top, axis=0, keepdims=True), (8, ROWS))
 
     def add_terms(a, terms, slots):
         for n, (j, half) in enumerate(chunks):
@@ -166,22 +166,27 @@
         q, g = part(2, 0, i), part(3, 0, i)
         gt = g.T
         slots = slots_of(i)
-        top = t_refs[buf][0:1]
-        total = jnp.zeros((1, ROWS), F32)
+        top = t_refs[buf][...]
+        total = jnp.zeros((8, ROWS), F32)
         for n in range(len(chunks)):
-            e = jnp.exp2((s_ref[rows[n]] - top) * power)
-            s_ref[rows[n]] = e
-            total = total + jnp.sum(e, axis=0, keepdims=True)
-        inverse = 1.0 / total
+            e = jnp.exp2((s_ref[rows[n]].reshape(ROWS // 8, 8, ROWS) - top) * power)
+            s_ref[rows[n]] = e.reshape(ROWS, ROWS)
+            total = total + jnp.sum(e, axis=0)
+        t_refs[buf][...] = jnp.broadcast_to(1.0 / jnp.sum(total, axis=0, keepdims=True), (8, ROWS))
+        inverse = t_refs[buf][...]
         for n in range(len(chunks)):
-            low_ref[rows[n]] = (s_ref[rows[n]] * inverse).astype(BF)
+            low = s_ref[rows[n]].reshape(ROWS // 8, 8, ROWS) * inverse
+            low_ref[rows[n]] = low.reshape(ROWS, ROWS).astype(BF)
         out_t = dot(flat(vt_ref, slots), low_ref[...])
         add_terms(1, dot(low_ref[...], g), slots)
         out = out_t.T.astype(BF)
         delta = jnp.sum(gt.astype(F32) * out_t.astype(BF).astype(F32), axis=0, keepdims=True)
+        d_ref[...] = jnp.broadcast_to(delta, (8, ROWS))
+        delta = d_ref[...]
         for n, (j, half) in enumerate(chunks):
-            dp = dot(part(1, half, slots[j]), gt)
-            ds_ref[rows[n]] = (s_ref[rows[n]] * inverse * (dp - delta)).astype(BF)
+            dp = dot(part(1, half, slots[j]), gt).reshape(ROWS // 8, 8, ROWS)
+            ds = s_ref[rows[n]].reshape(ROWS // 8, 8, ROWS) * inverse * (dp - delta)
+            ds_ref[rows[n]] = ds.reshape(ROWS, ROWS).astype(BF)
         query_t = dot(flat(kt_ref, slots), ds_ref[...])
         add_terms(0, dot(ds_ref[...], q), slots)
         query = (query_t * scale).T.astype(BF)
@@ -258,6 +263,7 @@
             pltpu.VMEM((2 * nb, HD, ROWS), BF),
             pltpu.VMEM((KEYS, ROWS), F32),
             pltpu.VMEM((KEYS, ROWS), F32),
+            pltpu.VMEM((8, ROWS), F32),
             pltpu.VMEM((8, ROWS), F32),
             pltpu.VMEM((8, ROWS), F32),
             pltpu.VMEM((KEYS, ROWS), BF),
@@ -411,7 +417,7 @@
     own = lax.all_to_all(parts, CHIPS, 0, 0, tiled=True)
     n = own.shape[0]
     mine = cut_out(
-        "cut_keys", (n, 2, HALF, HD), 56,
+        "cut_keys", (n, 2, HALF, HD), 50,
         lambda _, refs: [
             (refs[0].at[pl.ds(g * n // 4, n // 4), 0:2], pl.ds(g * n // 4, n // 4)) for g in range(4)
         ],

time: 176 us -> 173 us (0.983)
  Pallas kernels: 51.1 us -> 48.4 us
    pallas_call x1, Pallas kernels: 33.8 us -> 31.9 us  [attend(): call(attend_kernel, 'attend_head', [jax.ShapeDtypeStruct((n, 3, HALF, HD)...]
where the time goes in v3:
time: 173 us; the launch traced here: 172 us
  blocking collectives  107 us (62%)
  Pallas kernels  48.4 us (28%)
  waiting for transfers between devices  9.04 us (5%)
  starting transfers between devices  6.68 us (4%)
    all_to_all x1, blocking collectives, on_device(): own = lax.all_to_all(parts, CHIPS, 0, 0, tiled=True)  62 us
    all_to_all x1, blocking collectives, on_device(): back = lax.all_to_all(whole, CHIPS, 0, 0, tiled=True)  45.2 us
    pallas_call x1, Pallas kernels, attend(): call(attend_kernel, 'attend_head', [jax.ShapeDtypeStruct((n, 3, HALF, HD)...  31.9 us
    pallas_call x3, Pallas kernels, cut_out(): call(kernel, name, jax.ShapeDtypeStruct(out_shape, BF), 1, len(sources),...  5.65 us
    pallas_call x2, Pallas kernels, gather(): call(kernel, 'gather_heads', [jax.ShapeDtypeStruct((1, 2 * HALF, heads *...  5.39 us
    pallas_call x2, Pallas kernels, spread(): call(kernel, 'spread_heads', jax.ShapeDtypeStruct((2 * WIDE, 4, HALF, HD)...  4.29 us
    ppermute x1, waiting for transfers between devices, on_device(): other = lax.ppermute(mine, 'pipe', SWAP)  3.83 us
    ppermute x1, waiting for transfers between devices, on_device(): whole = combine(first, mine, lax.ppermute(theirs, 'pipe', SWAP))  3.82 us
  transfers between devices with their start and end apart: 5, of which 5 were waited for; matrix products, arithmetic and copies ran while one was open for 0% of the time, Pallas kernels for 3%

profile of v3, /device:TPU:1, one launch (start us, length us, event | category | flops | bytes accessed | tf_op | source)
XLA Modules:
  0.0 172.4 jit_solution(11276902928441534090)
XLA Ops:
  0.6 0.0 copy-start
  0.6 2.4 %cut_tokens.1 = bf16[4,64,3584]{2,1,0:T(8,128)(2,1)} custom-call(s32[1]{0:T(128)} %bitcast.place_ref, bf16[1,128,3584]{2,1,0:T(8,128)(2,1)} %refs_0_.1, bf16[1,128,3584]{2,1,0:T(8,128)(2,1)} %refs_1_.1, bf16[1,128,3584]{2,1,0:T(8,128)(2,1)} %refs_2_.1, bf16[1,128,3584]{2,1,0:T(8,128)(2,1)} %refs_3_.1), custom_call_target="tpu_custom_call" | custom-call | bytes 2097152 | tf_op jit(solution)/shard_map/cut_tokens/pallas_call | solution.py:387
  3.0 1.5 collective-permute-start
  4.5 0.0 copy-done
  4.5 0.1 collective-permute-start.1
  4.6 0.1 pad_add_fusion.1.place_ref
  4.7 2.5 %spread_heads.2.refs_1_ = bf16[64,4,64,128]{3,2,1,0:T(8,128)(2,1)} custom-call(s32[1]{0:T(128)} %bitcast.place_ref, bf16[128,3584]{1,0:T(8,128)(2,1)} %bitcast.12, bf16[128,3584]{1,0:T(8,128)(2,1)} %bitcast.13, bf16[128,3584]{1,0:T(8,128)(2,1)} %bitcast.14, bf16[128,3584]{1,0:T(8,128)(2,1)} %bitcast.15), custom_call_target="tpu_custom_call" | custom-call | bytes 4194304 | tf_op jit(solution)/shard_map/spread_heads/pallas_call | solution.py:77
  7.2 0.6 collective-permute-done.1
  7.8 0.3 collective-permute-done.refs_0_
  8.1 1.8 %spread_heads.3 = bf16[64,4,64,128]{3,2,1,0:T(8,128)(2,1)} custom-call(s32[1]{0:T(128)} %bitcast.1.place_ref, bf16[4,64,3584]{2,1,0:T(8,128)(2,1)S(1)} %collective-permute-done.refs_0_, bf16[64,4,64,128]{3,2,1,0:T(8,128)(2,1)} %spread_heads.2.refs_1_), custom_call_target="tpu_custom_call", output_to_operand_aliasing={{}: (2, {})} | custom-call | bytes 4194304 | tf_op jit(solution)/shard_map/spread_heads/pallas_call | solution.py:77
  9.9 62.0 %all_to_all.10.refs_0_.own_hbm = bf16[64,4,64,128]{3,2,1,0:T(8,128)(2,1)} all-to-all(bf16[64,4,64,128]{3,2,1,0:T(8,128)(2,1)} %spread_heads.3), channel_id=1, replica_groups=mesh['pipe'=2,'ctx'=16,'tp'=4] {'ctx','tp'}, dimensions={0} | all-to-all | bytes 8388608 | tf_op jit(solution)/shard_map/all_to_all | solution.py:417
  71.9 1.6 cut_keys.1
  73.6 2.4 %collective-permute-start.2 = (bf16[64,2,64,128]{3,2,1,0:T(8,128)(2,1)S(1)}, bf16[64,2,64,128]{3,2,1,0:T(8,128)(2,1)}, u32[]{:S(2)}, u32[]{:S(2)}) collective-permute-start(bf16[64,2,64,128]{3,2,1,0:T(8,128)(2,1)S(1)} %cut_keys.1), channel_id=1, source_target_pairs={{0,64},{64,0},{1,65},{65,1},{2,66},{66,2},{3,67},{67,3},{4,68},{68... | collective-permute-start | bytes 6291464 | tf_op jit(solution)/shard_map/ppermute | solution.py:426
  76.0 0.1 copy.15.picks_ref
  76.1 3.8 %collective-permute-done.2.other_hbm = bf16[64,2,64,128]{3,2,1,0:T(8,128)(2,1)} collective-permute-done((bf16[64,2,64,128]{3,2,1,0:T(8,128)(2,1)S(1)}, bf16[64,2,64,128]{3,2,1,0:T(8,128)(2,1)}, u32[]{:S(2)}, u32[]{:S(2)}) %collective-permute-start.2) | collective-permute-done | bytes 2097184 | tf_op jit(solution)/shard_map/ppermute | solution.py:426
  79.9 31.9 %attend_head.1 = (bf16[64,3,64,128]{3,2,1,0:T(8,128)(2,1)S(1)}, f32[2,64,64,128]{3,2,1,0:T(8,128)S(1)}, bf16[2,64,64,128]{3,2,1,0:T(8,128)(2,1)S(1)}) custom-call(s32[2]{0:T(128)S(1)} %pad_add_fusion.1.place_ref, s32[16,3]{1,0:T(8,128)S(1)} %copy.15.picks_ref, bf16[64,4,64,128]{3,2,1,0:T(8,128)(2,1)} %all_to_all.10.refs_0_.own_hbm, ...), custom_call_target="tpu_custom_call" | custom-call | flops 12884901888 | bytes 16777216 | tf_op jit(solution)/shard_map/attend_head/pallas_call | solution.py:251
  111.8 0.4 collective-permute-start.3
  112.2 3.8 %collective-permute-done.3.got_hbm = bf16[2,64,64,128]{3,2,1,0:T(8,128)(2,1)S(1)} collective-permute-done((bf16[2,64,64,128]{3,2,1,0:T(8,128)(2,1)S(1)}, bf16[2,64,64,128]{3,2,1,0:T(8,128)(2,1)S(1)}, u32[]{:S(2)}, u32[]{:S(2)}) %collective-permute-start.3) | collective-permute-done | bytes 2097184 | tf_op jit(solution)/shard_map/ppermute | solution.py:428
  116.1 1.1 combine_halves.1
  117.2 45.2 %all_to_all.11.refs_0_.source_ref = bf16[64,3,64,128]{3,2,1,0:T(8,128)(2,1)S(1)} all-to-all(bf16[64,3,64,128]{3,2,1,0:T(8,128)(2,1)S(1)} %combine_halves.1), channel_id=1, replica_groups=mesh['pipe'=2,'ctx'=16,'tp'=4] {'ctx','tp'}, dimensions={0} | all-to-all | bytes 6291456 | tf_op jit(solution)/shard_map/all_to_all | solution.py:430
  162.4 1.7 cut_heads.1
  164.1 2.2 %collective-permute-start.4 = (bf16[28,3,64,128]{3,2,1,0:T(8,128)(2,1)}, bf16[28,3,64,128]{3,2,1,0:T(8,128)(2,1)}, u32[]{:S(2)}, u32[]{:S(2)}) collective-permute-start(bf16[28,3,64,128]{3,2,1,0:T(8,128)(2,1)} %cut_heads.1), channel_id=1, source_target_pairs={{0,64},{64,0},{1,65},{65,1},{2,66},{66,2},{3,67},{67,3},{4,68},{68... | collective-permute-start | bytes 4128776 | tf_op jit(solution)/shard_map/ppermute | solution.py:438
  166.3 0.1 pad_add_fusion.2.place_ref
  166.4 0.1 pad_add_fusion.place_ref
  166.5 2.5 %gather_heads.2 = (bf16[1,128,3584]{2,1,0:T(8,128)(2,1)}, bf16[1,128,3584]{2,1,0:T(8,128)(2,1)}, bf16[1,128,3584]{2,1,0:T(8,128)(2,1)}, bf16[1,128,3584]{2,1,0:T(8,128)(2,1)}) custom-call(s32[2]{0:T(128)S(1)} %pad_add_fusion.2.place_ref, bf16[64,3,64,128]{3,2,1,0:T(8,128)(2,1)S(1)} %all_to_all.11.refs_0_.source_ref), custom_call_target="tpu_custom_call" | custom-call | bytes 4194304 | tf_op jit(solution)/shard_map/gather_heads/pallas_call | solution.py:360
  169.0 0.5 collective-permute-done.4.source_ref
  169.4 2.9 %gather_heads.3 = (bf16[1,128,3584]{2,1,0:T(8,128)(2,1)}, bf16[1,128,3584]{2,1,0:T(8,128)(2,1)}, bf16[1,128,3584]{2,1,0:T(8,128)(2,1)}, bf16[1,128,3584]{2,1,0:T(8,128)(2,1)}) custom-call(s32[2]{0:T(128)S(1)} %pad_add_fusion.place_ref, ...), custom_call_target="tpu_custom_call", output_to_operand_aliasing={{0}: (2, {}), {1}: (3, {}), {2}: (4, {}), {3}: (5, {})} | custom-call | bytes 4194304 | tf_op jit(solution)/shard_map/gather_heads/pallas_call | solution.py:360
  (2 shorter events, 0.0 us)
Async XLA Ops:
  0.6 3.9 %copy-start = (s32[1,16,3]{1,0,2:T(1,128)S(1)}, s32[1,16,3]{1,0,2:T(1,128)}, u32[]{:S(2)}) copy-start(s32[1,16,3]{1,0,2:T(1,128)} %param.9) | copy-start | bytes 580
  3.0 5.1 %collective-permute-start = (bf16[4,64,3584]{2,1,0:T(8,128)(2,1)}, bf16[4,64,3584]{2,1,0:T(8,128)(2,1)S(1)}, u32[]{:S(2)}, u32[]{:S(2)}) collective-permute-start(bf16[4,64,3584]{2,1,0:T(8,128)(2,1)} %cut_tokens.1), channel_id=1, source_target_pairs={{0,64},{64,0},{1,65},{65,1},{2,66},{66,2},{3,67},{67,3},{4,68},{68... | collective-permute-start | bytes 5505032 | tf_op jit(solution)/shard_map/ppermute | solution.py:410
  4.5 3.3 %collective-permute-start.1 = (s32[1,16,3]{1,0,2:T(1,128)S(1)}, s32[1,16,3]{1,0,2:T(1,128)S(1)}, u32[]{:S(2)}, u32[]{:S(2)}) collective-permute-start(s32[1,16,3]{1,0,2:T(1,128)S(1)} %copy-done), channel_id=1, source_target_pairs={{0,64},{64,0},{1,65},{65,1},{2,66},{66,2},{3,67},{67,3},{4,68},{68... | collective-permute-start | bytes 584 | tf_op jit(solution)/shard_map/ppermute | solution.py:411
  73.6 6.3 %collective-permute-start.2 = (bf16[64,2,64,128]{3,2,1,0:T(8,128)(2,1)S(1)}, bf16[64,2,64,128]{3,2,1,0:T(8,128)(2,1)}, u32[]{:S(2)}, u32[]{:S(2)}) collective-permute-start(bf16[64,2,64,128]{3,2,1,0:T(8,128)(2,1)S(1)} %cut_keys.1), channel_id=1, source_target_pairs={{0,64},{64,0},{1,65},{65,1},{2,66},{66,2},{3,67},{67,3},{4,68},{68... | collective-permute-start | bytes 6291464 | tf_op jit(solution)/shard_map/ppermute | solution.py:426
  111.8 4.2 %collective-permute-start.3 = (bf16[2,64,64,128]{3,2,1,0:T(8,128)(2,1)S(1)}, bf16[2,64,64,128]{3,2,1,0:T(8,128)(2,1)S(1)}, u32[]{:S(2)}, u32[]{:S(2)}) collective-permute-start(bf16[2,64,64,128]{3,2,1,0:T(8,128)(2,1)S(1)} %get-tuple-element.19), channel_id=1, source_target_pairs={{0,64},{64,0},{1,65},{65,1},{2,66},{66,2},{3,67},{67,3},{4,68},{68... | collective-permute-start | bytes 6291464 | tf_op jit(solution)/shard_map/ppermute | solution.py:428
  164.1 5.3 %collective-permute-start.4 = (bf16[28,3,64,128]{3,2,1,0:T(8,128)(2,1)}, bf16[28,3,64,128]{3,2,1,0:T(8,128)(2,1)}, u32[]{:S(2)}, u32[]{:S(2)}) collective-permute-start(bf16[28,3,64,128]{3,2,1,0:T(8,128)(2,1)} %cut_heads.1), channel_id=1, source_target_pairs={{0,64},{64,0},{1,65},{65,1},{2,66},{66,2},{3,67},{67,3},{4,68},{68... | collective-permute-start | bytes 4128776 | tf_op jit(solution)/shard_map/ppermute | solution.py:438

commit v4 on v3

--- a/solution.py
+++ b/solution.py
@@ -98,7 +98,7 @@
     scale = 1.0 / math.sqrt(HD)
     power = scale * math.log2(math.e)
     s_refs, t_refs = (s0_ref, s1_ref), (t0_ref, t1_ref)
-    chunks = [(j, half) for j in range(TOPK + 1) for half in range(2)]
+    chunks = [(j, half) for half in range(2) for j in range(TOPK + 1)]
     rows = [pl.ds(n * ROWS, ROWS) for n in range(len(chunks))]
 
     def loads(b):
@@ -369,24 +369,28 @@
     )(jnp.stack([core, base]), source, *extra)
 
 
-def cut_out(name, out_shape, vmem, pieces, place, *sources):
+def cut_out(name, out_shape, vmem, pieces, place, *sources, direct=False):
     def kernel(place_ref, *refs):
         out_ref, held, in_sem, out_sem = refs[-4:]
-        copies = []
+        first, then = [], []
         for n, (src, at) in enumerate(pieces(place_ref, refs[:-4])):
-            there = pltpu.make_async_copy(src, held.at[at], in_sem.at[n])
-            copies.append((there, pltpu.make_async_copy(held.at[at], out_ref.at[at], out_sem.at[n])))
-        for there, _ in copies:
-            there.start()
-        for there, back in copies:
-            there.wait()
-            back.start()
-        for _, back in copies:
-            back.wait()
+            if direct:
+                first.append(pltpu.make_async_copy(src, out_ref.at[at], in_sem.at[n]))
+            else:
+                first.append(pltpu.make_async_copy(src, held.at[at], in_sem.at[n]))
+                then.append(pltpu.make_async_copy(held.at[at], out_ref.at[at], out_sem.at[n]))
+        for copy in first:
+            copy.start()
+        for n, copy in enumerate(first):
+            copy.wait()
+            if not direct:
+                then[n].start()
+        for copy in then:
+            copy.wait()
 
     return call(
         kernel, name, jax.ShapeDtypeStruct(out_shape, BF), 1, len(sources),
-        [pltpu.VMEM(out_shape, BF), pltpu.SemaphoreType.DMA((4,)), pltpu.SemaphoreType.DMA((4,))],
+        [pltpu.VMEM((8, HD) if direct else out_shape, BF), pltpu.SemaphoreType.DMA((4,)), pltpu.SemaphoreType.DMA((4,))],
         vmem, 2 << 20,
     )(place[None], *sources)
 
@@ -433,7 +437,7 @@
         lambda place_ref, refs: [
             (refs[0].at[pl.ds(place_ref[0] * WIDE + g * GROUP, GROUP)], pl.ds(g * GROUP, GROUP)) for g in range(4)
         ],
-        core, back,
+        core, back, direct=True,
     )
     got = lax.ppermute(theirs, "pipe", SWAP)
     results = gather(core, back, (1 - core) * WIDE, True)

time: 173 us -> 172 us (level)
  no operation moved by 1% of the time
where the time goes in v4:
time: 172 us; the launch traced here: 171 us
  blocking collectives  107 us (62%)
  Pallas kernels  47.5 us (28%)
  waiting for transfers between devices  9.01 us (5%)
  starting transfers between devices  6.71 us (4%)
    all_to_all x1, blocking collectives, on_device(): own = lax.all_to_all(parts, CHIPS, 0, 0, tiled=True)  62 us
    all_to_all x1, blocking collectives, on_device(): back = lax.all_to_all(whole, CHIPS, 0, 0, tiled=True)  45.2 us
    pallas_call x1, Pallas kernels, attend(): call(attend_kernel, 'attend_head', [jax.ShapeDtypeStruct((n, 3, HALF, HD)...  31.5 us
    pallas_call x2, Pallas kernels, gather(): call(kernel, 'gather_heads', [jax.ShapeDtypeStruct((1, 2 * HALF, heads *...  5.39 us
    pallas_call x3, Pallas kernels, cut_out(): call(kernel, name, jax.ShapeDtypeStruct(out_shape, BF), 1, len(sources),...  5.16 us
    pallas_call x2, Pallas kernels, spread(): call(kernel, 'spread_heads', jax.ShapeDtypeStruct((2 * WIDE, 4, HALF, HD)...  4.29 us
    ppermute x1, waiting for transfers between devices, on_device(): other = lax.ppermute(mine, 'pipe', SWAP)  3.83 us
    ppermute x1, waiting for transfers between devices, on_device(): whole = combine(first, mine, lax.ppermute(theirs, 'pipe', SWAP))  3.79 us
  transfers between devices with their start and end apart: 5, of which 5 were waited for; matrix products, arithmetic and copies ran while one was open for 0% of the time, Pallas kernels for 3%

profile of v4, /device:TPU:1, one launch (start us, length us, event | category | flops | bytes accessed | tf_op | source)
XLA Modules:
  0.0 171.5 jit_solution(18247395846905049445)
XLA Ops:
  0.6 0.0 copy-start
  0.6 2.4 %cut_tokens.1 = bf16[4,64,3584]{2,1,0:T(8,128)(2,1)} custom-call(s32[1]{0:T(128)} %bitcast.place_ref, bf16[1,128,3584]{2,1,0:T(8,128)(2,1)} %refs_0_.1, bf16[1,128,3584]{2,1,0:T(8,128)(2,1)} %refs_1_.1, bf16[1,128,3584]{2,1,0:T(8,128)(2,1)} %refs_2_.1, bf16[1,128,3584]{2,1,0:T(8,128)(2,1)} %refs_3_.1), custom_call_target="tpu_custom_call" | custom-call | bytes 2097152 | tf_op jit(solution)/shard_map/cut_tokens/pallas_call | solution.py:391
  3.0 1.5 collective-permute-start
  4.5 0.0 copy-done
  4.5 0.1 collective-permute-start.1
  4.6 0.1 pad_add_fusion.1.place_ref
  4.7 2.5 %spread_heads.2.refs_1_ = bf16[64,4,64,128]{3,2,1,0:T(8,128)(2,1)} custom-call(s32[1]{0:T(128)} %bitcast.place_ref, bf16[128,3584]{1,0:T(8,128)(2,1)} %bitcast.12, bf16[128,3584]{1,0:T(8,128)(2,1)} %bitcast.13, bf16[128,3584]{1,0:T(8,128)(2,1)} %bitcast.14, bf16[128,3584]{1,0:T(8,128)(2,1)} %bitcast.15), custom_call_target="tpu_custom_call" | custom-call | bytes 4194304 | tf_op jit(solution)/shard_map/spread_heads/pallas_call | solution.py:77
  7.2 0.6 collective-permute-done.1
  7.8 0.3 collective-permute-done.refs_0_
  8.1 1.8 %spread_heads.3 = bf16[64,4,64,128]{3,2,1,0:T(8,128)(2,1)} custom-call(s32[1]{0:T(128)} %bitcast.1.place_ref, bf16[4,64,3584]{2,1,0:T(8,128)(2,1)S(1)} %collective-permute-done.refs_0_, bf16[64,4,64,128]{3,2,1,0:T(8,128)(2,1)} %spread_heads.2.refs_1_), custom_call_target="tpu_custom_call", output_to_operand_aliasing={{}: (2, {})} | custom-call | bytes 4194304 | tf_op jit(solution)/shard_map/spread_heads/pallas_call | solution.py:77
  9.9 62.0 %all_to_all.10.refs_0_.own_hbm = bf16[64,4,64,128]{3,2,1,0:T(8,128)(2,1)} all-to-all(bf16[64,4,64,128]{3,2,1,0:T(8,128)(2,1)} %spread_heads.3), channel_id=1, replica_groups=mesh['pipe'=2,'ctx'=16,'tp'=4] {'ctx','tp'}, dimensions={0} | all-to-all | bytes 8388608 | tf_op jit(solution)/shard_map/all_to_all | solution.py:421
  71.9 1.6 cut_keys.1
  73.6 2.4 %collective-permute-start.2 = (bf16[64,2,64,128]{3,2,1,0:T(8,128)(2,1)S(1)}, bf16[64,2,64,128]{3,2,1,0:T(8,128)(2,1)}, u32[]{:S(2)}, u32[]{:S(2)}) collective-permute-start(bf16[64,2,64,128]{3,2,1,0:T(8,128)(2,1)S(1)} %cut_keys.1), channel_id=1, source_target_pairs={{0,64},{64,0},{1,65},{65,1},{2,66},{66,2},{3,67},{67,3},{4,68},{68... | collective-permute-start | bytes 6291464 | tf_op jit(solution)/shard_map/ppermute | solution.py:430
  76.0 0.1 copy.15.picks_ref
  76.1 3.8 %collective-permute-done.2.other_hbm = bf16[64,2,64,128]{3,2,1,0:T(8,128)(2,1)} collective-permute-done((bf16[64,2,64,128]{3,2,1,0:T(8,128)(2,1)S(1)}, bf16[64,2,64,128]{3,2,1,0:T(8,128)(2,1)}, u32[]{:S(2)}, u32[]{:S(2)}) %collective-permute-start.2) | collective-permute-done | bytes 2097184 | tf_op jit(solution)/shard_map/ppermute | solution.py:430
  79.9 31.5 %attend_head.1 = (bf16[64,3,64,128]{3,2,1,0:T(8,128)(2,1)S(1)}, f32[2,64,64,128]{3,2,1,0:T(8,128)S(1)}, bf16[2,64,64,128]{3,2,1,0:T(8,128)(2,1)S(1)}) custom-call(s32[2]{0:T(128)S(1)} %pad_add_fusion.1.place_ref, s32[16,3]{1,0:T(8,128)S(1)} %copy.15.picks_ref, bf16[64,4,64,128]{3,2,1,0:T(8,128)(2,1)} %all_to_all.10.refs_0_.own_hbm, ...), custom_call_target="tpu_custom_call" | custom-call | flops 12884901888 | bytes 16777216 | tf_op jit(solution)/shard_map/attend_head/pallas_call | solution.py:251
  111.4 0.4 collective-permute-start.3
  111.8 3.8 %collective-permute-done.3.got_hbm = bf16[2,64,64,128]{3,2,1,0:T(8,128)(2,1)S(1)} collective-permute-done((bf16[2,64,64,128]{3,2,1,0:T(8,128)(2,1)S(1)}, bf16[2,64,64,128]{3,2,1,0:T(8,128)(2,1)S(1)}, u32[]{:S(2)}, u32[]{:S(2)}) %collective-permute-start.3) | collective-permute-done | bytes 2097184 | tf_op jit(solution)/shard_map/ppermute | solution.py:432
  115.6 1.1 combine_halves.1
  116.8 45.2 %all_to_all.11.refs_0_.source_ref = bf16[64,3,64,128]{3,2,1,0:T(8,128)(2,1)S(1)} all-to-all(bf16[64,3,64,128]{3,2,1,0:T(8,128)(2,1)S(1)} %combine_halves.1), channel_id=1, replica_groups=mesh['pipe'=2,'ctx'=16,'tp'=4] {'ctx','tp'}, dimensions={0} | all-to-all | bytes 6291456 | tf_op jit(solution)/shard_map/all_to_all | solution.py:434
  162.0 1.2 cut_heads.1
  163.2 2.2 %collective-permute-start.4 = (bf16[28,3,64,128]{3,2,1,0:T(8,128)(2,1)}, bf16[28,3,64,128]{3,2,1,0:T(8,128)(2,1)}, u32[]{:S(2)}, u32[]{:S(2)}) collective-permute-start(bf16[28,3,64,128]{3,2,1,0:T(8,128)(2,1)} %cut_heads.1), channel_id=1, source_target_pairs={{0,64},{64,0},{1,65},{65,1},{2,66},{66,2},{3,67},{67,3},{4,68},{68... | collective-permute-start | bytes 4128776 | tf_op jit(solution)/shard_map/ppermute | solution.py:442
  165.4 0.1 pad_add_fusion.2.place_ref
  165.5 0.1 pad_add_fusion.place_ref
  165.6 2.5 %gather_heads.2 = (bf16[1,128,3584]{2,1,0:T(8,128)(2,1)}, bf16[1,128,3584]{2,1,0:T(8,128)(2,1)}, bf16[1,128,3584]{2,1,0:T(8,128)(2,1)}, bf16[1,128,3584]{2,1,0:T(8,128)(2,1)}) custom-call(s32[2]{0:T(128)S(1)} %pad_add_fusion.2.place_ref, bf16[64,3,64,128]{3,2,1,0:T(8,128)(2,1)S(1)} %all_to_all.11.refs_0_.source_ref), custom_call_target="tpu_custom_call" | custom-call | bytes 4194304 | tf_op jit(solution)/shard_map/gather_heads/pallas_call | solution.py:360
  168.0 0.5 collective-permute-done.4.source_ref
  168.5 2.9 %gather_heads.3 = (bf16[1,128,3584]{2,1,0:T(8,128)(2,1)}, bf16[1,128,3584]{2,1,0:T(8,128)(2,1)}, bf16[1,128,3584]{2,1,0:T(8,128)(2,1)}, bf16[1,128,3584]{2,1,0:T(8,128)(2,1)}) custom-call(s32[2]{0:T(128)S(1)} %pad_add_fusion.place_ref, ...), custom_call_target="tpu_custom_call", output_to_operand_aliasing={{0}: (2, {}), {1}: (3, {}), {2}: (4, {}), {3}: (5, {})} | custom-call | bytes 4194304 | tf_op jit(solution)/shard_map/gather_heads/pallas_call | solution.py:360
  (2 shorter events, 0.0 us)
Async XLA Ops:
  0.6 3.9 %copy-start = (s32[1,16,3]{1,0,2:T(1,128)S(1)}, s32[1,16,3]{1,0,2:T(1,128)}, u32[]{:S(2)}) copy-start(s32[1,16,3]{1,0,2:T(1,128)} %param.9) | copy-start | bytes 580
  3.0 5.1 %collective-permute-start = (bf16[4,64,3584]{2,1,0:T(8,128)(2,1)}, bf16[4,64,3584]{2,1,0:T(8,128)(2,1)S(1)}, u32[]{:S(2)}, u32[]{:S(2)}) collective-permute-start(bf16[4,64,3584]{2,1,0:T(8,128)(2,1)} %cut_tokens.1), channel_id=1, source_target_pairs={{0,64},{64,0},{1,65},{65,1},{2,66},{66,2},{3,67},{67,3},{4,68},{68... | collective-permute-start | bytes 5505032 | tf_op jit(solution)/shard_map/ppermute | solution.py:414
  4.5 3.3 %collective-permute-start.1 = (s32[1,16,3]{1,0,2:T(1,128)S(1)}, s32[1,16,3]{1,0,2:T(1,128)S(1)}, u32[]{:S(2)}, u32[]{:S(2)}) collective-permute-start(s32[1,16,3]{1,0,2:T(1,128)S(1)} %copy-done), channel_id=1, source_target_pairs={{0,64},{64,0},{1,65},{65,1},{2,66},{66,2},{3,67},{67,3},{4,68},{68... | collective-permute-start | bytes 584 | tf_op jit(solution)/shard_map/ppermute | solution.py:415
  73.6 6.3 %collective-permute-start.2 = (bf16[64,2,64,128]{3,2,1,0:T(8,128)(2,1)S(1)}, bf16[64,2,64,128]{3,2,1,0:T(8,128)(2,1)}, u32[]{:S(2)}, u32[]{:S(2)}) collective-permute-start(bf16[64,2,64,128]{3,2,1,0:T(8,128)(2,1)S(1)} %cut_keys.1), channel_id=1, source_target_pairs={{0,64},{64,0},{1,65},{65,1},{2,66},{66,2},{3,67},{67,3},{4,68},{68... | collective-permute-start | bytes 6291464 | tf_op jit(solution)/shard_map/ppermute | solution.py:430
  111.4 4.2 %collective-permute-start.3 = (bf16[2,64,64,128]{3,2,1,0:T(8,128)(2,1)S(1)}, bf16[2,64,64,128]{3,2,1,0:T(8,128)(2,1)S(1)}, u32[]{:S(2)}, u32[]{:S(2)}) collective-permute-start(bf16[2,64,64,128]{3,2,1,0:T(8,128)(2,1)S(1)} %get-tuple-element.19), channel_id=1, source_target_pairs={{0,64},{64,0},{1,65},{65,1},{2,66},{66,2},{3,67},{67,3},{4,68},{68... | collective-permute-start | bytes 6291464 | tf_op jit(solution)/shard_map/ppermute | solution.py:432
  163.2 5.3 %collective-permute-start.4 = (bf16[28,3,64,128]{3,2,1,0:T(8,128)(2,1)}, bf16[28,3,64,128]{3,2,1,0:T(8,128)(2,1)}, u32[]{:S(2)}, u32[]{:S(2)}) collective-permute-start(bf16[28,3,64,128]{3,2,1,0:T(8,128)(2,1)} %cut_heads.1), channel_id=1, source_target_pairs={{0,64},{64,0},{1,65},{65,1},{2,66},{66,2},{3,67},{67,3},{4,68},{68... | collective-permute-start | bytes 4128776 | tf_op jit(solution)/shard_map/ppermute | solution.py:442

commit v5 on v4

--- a/solution.py
+++ b/solution.py
@@ -101,20 +101,17 @@
     chunks = [(j, half) for half in range(2) for j in range(TOPK + 1)]
     rows = [pl.ds(n * ROWS, ROWS) for n in range(len(chunks))]
 
-    def loads(b):
-        at = pl.ds(b * PART, PART)
+    edges = (0, 1, 3, 9, nb)
+
+    def loads(k):
+        at = pl.ds(edges[k] * PART, (edges[k + 1] - edges[k]) * PART)
         return (
-            pltpu.make_async_copy(own_hbm.at[at], own_ref.at[at], in_sem.at[b, 0]),
-            pltpu.make_async_copy(other_hbm.at[at], other_ref.at[at], in_sem.at[b, 1]),
+            pltpu.make_async_copy(own_hbm.at[at], own_ref.at[at], in_sem.at[k, 0]),
+            pltpu.make_async_copy(other_hbm.at[at], other_ref.at[at], in_sem.at[k, 1]),
         )
 
-    def start(b, carry):
-        for copy in loads(b):
-            copy.start()
-        return carry
-
-    def arrive(b):
-        for copy in loads(b):
+    def arrive(k):
+        for copy in loads(k):
             copy.wait()
 
     def part(a, half, b):
@@ -179,7 +176,7 @@
             low_ref[rows[n]] = low.reshape(ROWS, ROWS).astype(BF)
         out_t = dot(flat(vt_ref, slots), low_ref[...])
         add_terms(1, dot(low_ref[...], g), slots)
-        out = out_t.T.astype(BF)
+        out = out_t.astype(BF).T
         delta = jnp.sum(gt.astype(F32) * out_t.astype(BF).astype(F32), axis=0, keepdims=True)
         d_ref[...] = jnp.broadcast_to(delta, (8, ROWS))
         delta = d_ref[...]
@@ -189,7 +186,7 @@
             ds_ref[rows[n]] = ds.reshape(ROWS, ROWS).astype(BF)
         query_t = dot(flat(kt_ref, slots), ds_ref[...])
         add_terms(0, dot(ds_ref[...], q), slots)
-        query = (query_t * scale).T.astype(BF)
+        query = (query_t * scale).astype(BF).T
         first = jnp.where(seg == 0, out.astype(F32), query.astype(F32)).astype(BF)
         first_ref[pl.ds(i * PART, PART)] = first.reshape(PART, HALF, HD)
 
@@ -197,7 +194,9 @@
         at = pl.ds(p * 2 * PART, 2 * PART)
         return pltpu.make_async_copy(first_ref.at[at], first_hbm.at[at, 0], first_sem.at[p])
 
-    lax.fori_loop(0, nb, start, 0)
+    for k in range(len(edges) - 1):
+        for copy in loads(k):
+            copy.start()
     arrive(0)
     turn(0)
     scores(0, 0)
@@ -205,11 +204,12 @@
     def pair(p, carry):
         i = 2 * p
         later = jnp.minimum(i + 2, nb - 1)
-        arrive(i + 1)
-
-        @pl.when(i + 2 < nb)
-        def _():
-            arrive(i + 2)
+
+        for k in range(1, len(edges) - 1):
+
+            @pl.when(i + 1 == edges[k])
+            def _(k=k):
+                arrive(k)
 
         turn(i + 1)
         turn(later)
@@ -272,7 +272,7 @@
             pltpu.VMEM((2, n, HALF, HD), F32),
             pltpu.VMEM((2, n, HALF, HD), BF),
             pltpu.VMEM((n, HALF, HD), BF),
-            pltpu.SemaphoreType.DMA((nb, 2)),
+            pltpu.SemaphoreType.DMA((4, 2)),
             pltpu.SemaphoreType.DMA((nb // 2,)),
             pltpu.SemaphoreType.DMA((2,)),
             pltpu.SemaphoreType.DMA((nb // 4,)),
@@ -415,10 +415,11 @@
     other_chosen = lax.ppermute(chosen, "pipe", SWAP)
     parts = spread(core, [x[0] for x in arrays], core)
     parts = spread(core, [got], 1 - core, parts)
+    parts, other_chosen = lax.optimization_barrier((parts, other_chosen))
+
+    own = lax.all_to_all(parts, CHIPS, 0, 0, tiled=True)
+    own, other_chosen = lax.optimization_barrier((own, other_chosen))
     picks = jnp.where(seg == core, chosen, other_chosen)[0]
-    parts, picks, place = lax.optimization_barrier((parts, picks, place))
-
-    own = lax.all_to_all(parts, CHIPS, 0, 0, tiled=True)
     n = own.shape[0]
     mine = cut_out(
         "cut_keys", (n, 2, HALF, HD), 50,

time: 172 us -> 171 us (level)
  transfers between devices with their start and end apart: 5 -> 5, of which waited for: 5 -> 4; matrix products, arithmetic and copies ran while one was open for 0% -> 0% of each run, Pallas kernels for 3% -> 4%
where the time goes in v5:
time: 171 us
  blocking collectives  107 us (63%)
  Pallas kernels  47.1 us (28%)
  waiting for transfers between devices  9.01 us (5%)
  starting transfers between devices  6.71 us (4%)
    all_to_all x1, blocking collectives, on_device(): own = lax.all_to_all(parts, CHIPS, 0, 0, tiled=True)  62 us
    all_to_all x1, blocking collectives, on_device(): back = lax.all_to_all(whole, CHIPS, 0, 0, tiled=True)  45.2 us
    pallas_call x1, Pallas kernels, attend(): call(attend_kernel, 'attend_head', [jax.ShapeDtypeStruct((n, 3, HALF, HD)...  31.1 us
    pallas_call x2, Pallas kernels, gather(): call(kernel, 'gather_heads', [jax.ShapeDtypeStruct((1, 2 * HALF, heads *...  5.39 us
    pallas_call x3, Pallas kernels, cut_out(): call(kernel, name, jax.ShapeDtypeStruct(out_shape, BF), 1, len(sources),...  5.16 us
    pallas_call x2, Pallas kernels, spread(): call(kernel, 'spread_heads', jax.ShapeDtypeStruct((2 * WIDE, 4, HALF, HD)...  4.29 us
    ppermute x1, waiting for transfers between devices, on_device(): whole = combine(first, mine, lax.ppermute(theirs, 'pipe', SWAP))  3.79 us
    ppermute x1, waiting for transfers between devices, on_device(): other = lax.ppermute(mine, 'pipe', SWAP)  3.75 us
  transfers between devices with their start and end apart: 5, of which 4 were waited for; matrix products, arithmetic and copies ran while one was open for 0% of the time, Pallas kernels for 4%

profile of v5, /device:TPU:1, one launch (start us, length us, event | category | flops | bytes accessed | tf_op | source)
XLA Modules:
  0.0 171.1 jit_solution(6272907133363326116)
XLA Ops:
  0.6 0.0 copy-start
  0.6 2.4 %cut_tokens.1 = bf16[4,64,3584]{2,1,0:T(8,128)(2,1)} custom-call(s32[1]{0:T(128)} %bitcast.place_ref, bf16[1,128,3584]{2,1,0:T(8,128)(2,1)} %refs_0_.1, bf16[1,128,3584]{2,1,0:T(8,128)(2,1)} %refs_1_.1, bf16[1,128,3584]{2,1,0:T(8,128)(2,1)} %refs_2_.1, bf16[1,128,3584]{2,1,0:T(8,128)(2,1)} %refs_3_.1), custom_call_target="tpu_custom_call" | custom-call | bytes 2097152 | tf_op jit(solution)/shard_map/cut_tokens/pallas_call | solution.py:391
  3.0 1.5 collective-permute-start
  4.5 0.0 copy-done
  4.5 0.1 collective-permute-start.1
  4.6 2.5 %spread_heads.2.refs_1_ = bf16[64,4,64,128]{3,2,1,0:T(8,128)(2,1)} custom-call(s32[1]{0:T(128)} %bitcast.place_ref, bf16[128,3584]{1,0:T(8,128)(2,1)} %bitcast.11, bf16[128,3584]{1,0:T(8,128)(2,1)} %bitcast.12, bf16[128,3584]{1,0:T(8,128)(2,1)} %bitcast.13, bf16[128,3584]{1,0:T(8,128)(2,1)} %bitcast.14), custom_call_target="tpu_custom_call" | custom-call | bytes 4194304 | tf_op jit(solution)/shard_map/spread_heads/pallas_call | solution.py:77
  7.1 1.0 collective-permute-done.refs_0_
  8.1 1.8 %spread_heads.3 = bf16[64,4,64,128]{3,2,1,0:T(8,128)(2,1)} custom-call(s32[1]{0:T(128)} %bitcast.3.place_ref, bf16[4,64,3584]{2,1,0:T(8,128)(2,1)S(1)} %collective-permute-done.refs_0_, bf16[64,4,64,128]{3,2,1,0:T(8,128)(2,1)} %spread_heads.2.refs_1_), custom_call_target="tpu_custom_call", output_to_operand_aliasing={{}: (2, {})} | custom-call | bytes 4194304 | tf_op jit(solution)/shard_map/spread_heads/pallas_call | solution.py:77
  9.9 0.0 collective-permute-done.1
  9.9 62.0 %all_to_all.10.refs_0_.own_hbm = bf16[64,4,64,128]{3,2,1,0:T(8,128)(2,1)} all-to-all(bf16[64,4,64,128]{3,2,1,0:T(8,128)(2,1)} %spread_heads.3), channel_id=1, replica_groups=mesh['pipe'=2,'ctx'=16,'tp'=4] {'ctx','tp'}, dimensions={0} | all-to-all | bytes 8388608 | tf_op jit(solution)/shard_map/all_to_all | solution.py:420
  72.0 1.6 cut_keys.1
  73.6 2.4 %collective-permute-start.2 = (bf16[64,2,64,128]{3,2,1,0:T(8,128)(2,1)S(1)}, bf16[64,2,64,128]{3,2,1,0:T(8,128)(2,1)}, u32[]{:S(2)}, u32[]{:S(2)}) collective-permute-start(bf16[64,2,64,128]{3,2,1,0:T(8,128)(2,1)S(1)} %cut_keys.1), channel_id=1, source_target_pairs={{0,64},{64,0},{1,65},{65,1},{2,66},{66,2},{3,67},{67,3},{4,68},{68... | collective-permute-start | bytes 6291464 | tf_op jit(solution)/shard_map/ppermute | solution.py:431
  76.0 0.1 pad_add_fusion.1.place_ref
  76.1 0.1 copy.16
  76.2 3.8 %collective-permute-done.2.other_hbm = bf16[64,2,64,128]{3,2,1,0:T(8,128)(2,1)} collective-permute-done((bf16[64,2,64,128]{3,2,1,0:T(8,128)(2,1)S(1)}, bf16[64,2,64,128]{3,2,1,0:T(8,128)(2,1)}, u32[]{:S(2)}, u32[]{:S(2)}) %collective-permute-start.2) | collective-permute-done | bytes 2097184 | tf_op jit(solution)/shard_map/ppermute | solution.py:431
  79.9 31.1 %attend_head.1 = (bf16[64,3,64,128]{3,2,1,0:T(8,128)(2,1)S(1)}, f32[2,64,64,128]{3,2,1,0:T(8,128)S(1)}, bf16[2,64,64,128]{3,2,1,0:T(8,128)(2,1)S(1)}) custom-call(s32[2]{0:T(128)S(1)} %pad_add_fusion.1.place_ref, s32[16,3]{1,0:T(8,128)S(1)} %bitcast.10, bf16[64,4,64,128]{3,2,1,0:T(8,128)(2,1)} %all_to_all.10.refs_0_.own_hbm, ...), custom_call_target="tpu_custom_call" | custom-call | flops 12884901888 | bytes 16777216 | tf_op jit(solution)/shard_map/attend_head/pallas_call | solution.py:251
  111.1 0.5 collective-permute-start.3
  111.5 3.8 %collective-permute-done.3.got_hbm = bf16[2,64,64,128]{3,2,1,0:T(8,128)(2,1)S(1)} collective-permute-done((bf16[2,64,64,128]{3,2,1,0:T(8,128)(2,1)S(1)}, bf16[2,64,64,128]{3,2,1,0:T(8,128)(2,1)S(1)}, u32[]{:S(2)}, u32[]{:S(2)}) %collective-permute-start.3) | collective-permute-done | bytes 2097184 | tf_op jit(solution)/shard_map/ppermute | solution.py:433
  115.3 1.1 combine_halves.1
  116.4 45.2 %all_to_all.11.refs_0_.source_ref = bf16[64,3,64,128]{3,2,1,0:T(8,128)(2,1)S(1)} all-to-all(bf16[64,3,64,128]{3,2,1,0:T(8,128)(2,1)S(1)} %combine_halves.1), channel_id=1, replica_groups=mesh['pipe'=2,'ctx'=16,'tp'=4] {'ctx','tp'}, dimensions={0} | all-to-all | bytes 6291456 | tf_op jit(solution)/shard_map/all_to_all | solution.py:435
  161.6 1.2 cut_heads.1
  162.8 2.2 %collective-permute-start.4 = (bf16[28,3,64,128]{3,2,1,0:T(8,128)(2,1)}, bf16[28,3,64,128]{3,2,1,0:T(8,128)(2,1)}, u32[]{:S(2)}, u32[]{:S(2)}) collective-permute-start(bf16[28,3,64,128]{3,2,1,0:T(8,128)(2,1)} %cut_heads.1), channel_id=1, source_target_pairs={{0,64},{64,0},{1,65},{65,1},{2,66},{66,2},{3,67},{67,3},{4,68},{68... | collective-permute-start | bytes 4128776 | tf_op jit(solution)/shard_map/ppermute | solution.py:443
  165.1 0.1 pad_add_fusion.2.place_ref
  165.2 0.1 pad_add_fusion.place_ref
  165.2 2.5 %gather_heads.2 = (bf16[1,128,3584]{2,1,0:T(8,128)(2,1)}, bf16[1,128,3584]{2,1,0:T(8,128)(2,1)}, bf16[1,128,3584]{2,1,0:T(8,128)(2,1)}, bf16[1,128,3584]{2,1,0:T(8,128)(2,1)}) custom-call(s32[2]{0:T(128)S(1)} %pad_add_fusion.2.place_ref, bf16[64,3,64,128]{3,2,1,0:T(8,128)(2,1)S(1)} %all_to_all.11.refs_0_.source_ref), custom_call_target="tpu_custom_call" | custom-call | bytes 4194304 | tf_op jit(solution)/shard_map/gather_heads/pallas_call | solution.py:360
  167.7 0.5 collective-permute-done.4.source_ref
  168.2 2.9 %gather_heads.3 = (bf16[1,128,3584]{2,1,0:T(8,128)(2,1)}, bf16[1,128,3584]{2,1,0:T(8,128)(2,1)}, bf16[1,128,3584]{2,1,0:T(8,128)(2,1)}, bf16[1,128,3584]{2,1,0:T(8,128)(2,1)}) custom-call(s32[2]{0:T(128)S(1)} %pad_add_fusion.place_ref, ...), custom_call_target="tpu_custom_call", output_to_operand_aliasing={{0}: (2, {}), {1}: (3, {}), {2}: (4, {}), {3}: (5, {})} | custom-call | bytes 4194304 | tf_op jit(solution)/shard_map/gather_heads/pallas_call | solution.py:360
  (1 shorter events, 0.0 us)
Async XLA Ops:
  0.6 3.9 %copy-start = (s32[1,16,3]{1,0,2:T(1,128)S(1)}, s32[1,16,3]{1,0,2:T(1,128)}, u32[]{:S(2)}) copy-start(s32[1,16,3]{1,0,2:T(1,128)} %param.9) | copy-start | bytes 580
  3.0 5.1 %collective-permute-start = (bf16[4,64,3584]{2,1,0:T(8,128)(2,1)}, bf16[4,64,3584]{2,1,0:T(8,128)(2,1)S(1)}, u32[]{:S(2)}, u32[]{:S(2)}) collective-permute-start(bf16[4,64,3584]{2,1,0:T(8,128)(2,1)} %cut_tokens.1), channel_id=1, source_target_pairs={{0,64},{64,0},{1,65},{65,1},{2,66},{66,2},{3,67},{67,3},{4,68},{68... | collective-permute-start | bytes 5505032 | tf_op jit(solution)/shard_map/ppermute | solution.py:414
  4.5 5.4 %collective-permute-start.1 = (s32[1,16,3]{1,0,2:T(1,128)S(1)}, s32[1,16,3]{1,0,2:T(1,128)S(1)}, u32[]{:S(2)}, u32[]{:S(2)}) collective-permute-start(s32[1,16,3]{1,0,2:T(1,128)S(1)} %copy-done), channel_id=1, source_target_pairs={{0,64},{64,0},{1,65},{65,1},{2,66},{66,2},{3,67},{67,3},{4,68},{68... | collective-permute-start | bytes 584 | tf_op jit(solution)/shard_map/ppermute | solution.py:415
  73.6 6.3 %collective-permute-start.2 = (bf16[64,2,64,128]{3,2,1,0:T(8,128)(2,1)S(1)}, bf16[64,2,64,128]{3,2,1,0:T(8,128)(2,1)}, u32[]{:S(2)}, u32[]{:S(2)}) collective-permute-start(bf16[64,2,64,128]{3,2,1,0:T(8,128)(2,1)S(1)} %cut_keys.1), channel_id=1, source_target_pairs={{0,64},{64,0},{1,65},{65,1},{2,66},{66,2},{3,67},{67,3},{4,68},{68... | collective-permute-start | bytes 6291464 | tf_op jit(solution)/shard_map/ppermute | solution.py:431
  111.1 4.2 %collective-permute-start.3 = (bf16[2,64,64,128]{3,2,1,0:T(8,128)(2,1)S(1)}, bf16[2,64,64,128]{3,2,1,0:T(8,128)(2,1)S(1)}, u32[]{:S(2)}, u32[]{:S(2)}) collective-permute-start(bf16[2,64,64,128]{3,2,1,0:T(8,128)(2,1)S(1)} %get-tuple-element.21), channel_id=1, source_target_pairs={{0,64},{64,0},{1,65},{65,1},{2,66},{66,2},{3,67},{67,3},{4,68},{68... | collective-permute-start | bytes 6291464 | tf_op jit(solution)/shard_map/ppermute | solution.py:433
  162.8 5.3 %collective-permute-start.4 = (bf16[28,3,64,128]{3,2,1,0:T(8,128)(2,1)}, bf16[28,3,64,128]{3,2,1,0:T(8,128)(2,1)}, u32[]{:S(2)}, u32[]{:S(2)}) collective-permute-start(bf16[28,3,64,128]{3,2,1,0:T(8,128)(2,1)} %cut_heads.1), channel_id=1, source_target_pairs={{0,64},{64,0},{1,65},{65,1},{2,66},{66,2},{3,67},{67,3},{4,68},{68... | collective-permute-start | bytes 4128776 | tf_op jit(solution)/shard_map/ppermute | solution.py:443

commit v6 on v5

--- a/solution.py
+++ b/solution.py
@@ -331,8 +331,20 @@
     rows = slice(HALF, 2 * HALF) if high else slice(0, HALF)
 
     def kernel(place_ref, source_ref, *refs):
-        outs = refs[-8:-4]
-        got, cut, in_sem, out_sem = refs[-4:]
+        outs = refs[-10:-6]
+        got, cut, blank, in_sem, out_sem, blank_sem = refs[-6:]
+        live = [place_ref[0] == (1 if a == 0 else 0) for a in range(4)]
+
+        def clear(a):
+            return pltpu.make_async_copy(blank, outs[a].at[0, 0:HALF], blank_sem.at[a])
+
+        def fill(g, a):
+            for h in range(GROUP):
+                value = got[g, h, max(a - 1, 0)]
+                if high:
+                    value = jnp.where(live[a], value, jnp.zeros_like(value))
+                cut[g, a, :, h * HD : (h + 1) * HD] = value
+            store(g, a).start()
 
         def load(g):
             at = pl.ds(place_ref[1] + g * GROUP, GROUP)
@@ -347,14 +359,21 @@
         for g in range(groups):
             load(g).wait()
             for a in range(4):
-                live = place_ref[0] == (1 if a == 0 else 0)
-                for h in range(GROUP):
-                    value = got[g, h, max(a - 1, 0)]
-                    cut[g, a, :, h * HD : (h + 1) * HD] = jnp.where(live, value, jnp.zeros_like(value))
-                store(g, a).start()
-        for g in range(groups):
+                if high:
+                    fill(g, a)
+                else:
+                    pl.when(live[a])(lambda g=g, a=a: fill(g, a))
+        if high:
+            blank[...] = jnp.zeros_like(blank)
             for a in range(4):
-                store(g, a).wait()
+                pl.when(jnp.logical_not(live[a]))(lambda a=a: clear(a).start())
+        for a in range(4):
+            if high:
+                for g in range(groups):
+                    store(g, a).wait()
+                pl.when(jnp.logical_not(live[a]))(lambda a=a: clear(a).wait())
+            else:
+                pl.when(live[a])(lambda a=a: [store(g, a).wait() for g in range(groups)] and None)
 
     extra = [] if results is None else list(results)
     return call(
@@ -362,8 +381,10 @@
         [
             pltpu.VMEM((groups, GROUP, 3, HALF, HD), BF),
             pltpu.VMEM((groups, 4, HALF, GROUP * HD), BF),
+            pltpu.VMEM((HALF, heads * HD), BF),
             pltpu.SemaphoreType.DMA((groups,)),
             pltpu.SemaphoreType.DMA((groups, 4)),
+            pltpu.SemaphoreType.DMA((4,)),
         ],
         8, 4 << 20, aliases={2 + a: a for a in range(4)} if extra else None,
     )(jnp.stack([core, base]), source, *extra)

time: 171 us -> 171 us (level)
  transfers between devices with their start and end apart: 5 -> 5, of which waited for: 4 -> 3; matrix products, arithmetic and copies ran while one was open for 0% -> 0% of each run, Pallas kernels for 4% -> 4%
where the time goes in v6:
time: 171 us
  blocking collectives  107 us (63%)
  Pallas kernels  47.4 us (28%)
  waiting for transfers between devices  8.53 us (5%)
  starting transfers between devices  6.71 us (4%)
    all_to_all x1, blocking collectives, on_device(): own = lax.all_to_all(parts, CHIPS, 0, 0, tiled=True)  62 us
    all_to_all x1, blocking collectives, on_device(): back = lax.all_to_all(whole, CHIPS, 0, 0, tiled=True)  45.2 us
    pallas_call x1, Pallas kernels, attend(): call(attend_kernel, 'attend_head', [jax.ShapeDtypeStruct((n, 3, HALF, HD)...  31.1 us
    pallas_call x2, Pallas kernels, gather(): call(kernel, 'gather_heads', [jax.ShapeDtypeStruct((1, 2 * HALF, heads *...  5.67 us
    pallas_call x3, Pallas kernels, cut_out(): call(kernel, name, jax.ShapeDtypeStruct(out_shape, BF), 1, len(sources),...  5.16 us
    pallas_call x2, Pallas kernels, spread(): call(kernel, 'spread_heads', jax.ShapeDtypeStruct((2 * WIDE, 4, HALF, HD)...  4.29 us
    ppermute x1, waiting for transfers between devices, on_device(): whole = combine(first, mine, lax.ppermute(theirs, 'pipe', SWAP))  3.79 us
    ppermute x1, waiting for transfers between devices, on_device(): other = lax.ppermute(mine, 'pipe', SWAP)  3.75 us
  transfers between devices with their start and end apart: 5, of which 3 were waited for; matrix products, arithmetic and copies ran while one was open for 0% of the time, Pallas kernels for 4%

profile of v6, /device:TPU:1, one launch (start us, length us, event | category | flops | bytes accessed | tf_op | source)
XLA Modules:
  0.0 170.9 jit_solution(2468584960406971694)
XLA Ops:
  0.6 0.0 copy-start
  0.6 2.4 %cut_tokens.1 = bf16[4,64,3584]{2,1,0:T(8,128)(2,1)} custom-call(s32[1]{0:T(128)} %bitcast.place_ref, bf16[1,128,3584]{2,1,0:T(8,128)(2,1)} %refs_0_.1, bf16[1,128,3584]{2,1,0:T(8,128)(2,1)} %refs_1_.1, bf16[1,128,3584]{2,1,0:T(8,128)(2,1)} %refs_2_.1, bf16[1,128,3584]{2,1,0:T(8,128)(2,1)} %refs_3_.1), custom_call_target="tpu_custom_call" | custom-call | bytes 2097152 | tf_op jit(solution)/shard_map/cut_tokens/pallas_call | solution.py:412
  3.0 1.5 collective-permute-start
  4.5 0.0 copy-done
  4.5 0.1 collective-permute-start.1
  4.6 2.5 %spread_heads.2.refs_1_ = bf16[64,4,64,128]{3,2,1,0:T(8,128)(2,1)} custom-call(s32[1]{0:T(128)} %bitcast.place_ref, bf16[128,3584]{1,0:T(8,128)(2,1)} %bitcast.11, bf16[128,3584]{1,0:T(8,128)(2,1)} %bitcast.12, bf16[128,3584]{1,0:T(8,128)(2,1)} %bitcast.13, bf16[128,3584]{1,0:T(8,128)(2,1)} %bitcast.14), custom_call_target="tpu_custom_call" | custom-call | bytes 4194304 | tf_op jit(solution)/shard_map/spread_heads/pallas_call | solution.py:77
  7.1 1.0 collective-permute-done.refs_0_
  8.1 1.8 %spread_heads.3 = bf16[64,4,64,128]{3,2,1,0:T(8,128)(2,1)} custom-call(s32[1]{0:T(128)} %bitcast.3.place_ref, bf16[4,64,3584]{2,1,0:T(8,128)(2,1)S(1)} %collective-permute-done.refs_0_, bf16[64,4,64,128]{3,2,1,0:T(8,128)(2,1)} %spread_heads.2.refs_1_), custom_call_target="tpu_custom_call", output_to_operand_aliasing={{}: (2, {})} | custom-call | bytes 4194304 | tf_op jit(solution)/shard_map/spread_heads/pallas_call | solution.py:77
  9.9 0.0 collective-permute-done.1
  9.9 62.0 %all_to_all.10.refs_0_.own_hbm = bf16[64,4,64,128]{3,2,1,0:T(8,128)(2,1)} all-to-all(bf16[64,4,64,128]{3,2,1,0:T(8,128)(2,1)} %spread_heads.3), channel_id=1, replica_groups=mesh['pipe'=2,'ctx'=16,'tp'=4] {'ctx','tp'}, dimensions={0} | all-to-all | bytes 8388608 | tf_op jit(solution)/shard_map/all_to_all | solution.py:441
  72.0 1.6 cut_keys.1
  73.6 2.4 %collective-permute-start.2 = (bf16[64,2,64,128]{3,2,1,0:T(8,128)(2,1)S(1)}, bf16[64,2,64,128]{3,2,1,0:T(8,128)(2,1)}, u32[]{:S(2)}, u32[]{:S(2)}) collective-permute-start(bf16[64,2,64,128]{3,2,1,0:T(8,128)(2,1)S(1)} %cut_keys.1), channel_id=1, source_target_pairs={{0,64},{64,0},{1,65},{65,1},{2,66},{66,2},{3,67},{67,3},{4,68},{68... | collective-permute-start | bytes 6291464 | tf_op jit(solution)/shard_map/ppermute | solution.py:452
  76.0 0.1 pad_add_fusion.1.place_ref
  76.1 0.1 copy.16
  76.2 3.8 %collective-permute-done.2.other_hbm = bf16[64,2,64,128]{3,2,1,0:T(8,128)(2,1)} collective-permute-done((bf16[64,2,64,128]{3,2,1,0:T(8,128)(2,1)S(1)}, bf16[64,2,64,128]{3,2,1,0:T(8,128)(2,1)}, u32[]{:S(2)}, u32[]{:S(2)}) %collective-permute-start.2) | collective-permute-done | bytes 2097184 | tf_op jit(solution)/shard_map/ppermute | solution.py:452
  79.9 31.1 %attend_head.1 = (bf16[64,3,64,128]{3,2,1,0:T(8,128)(2,1)S(1)}, f32[2,64,64,128]{3,2,1,0:T(8,128)S(1)}, bf16[2,64,64,128]{3,2,1,0:T(8,128)(2,1)S(1)}) custom-call(s32[2]{0:T(128)S(1)} %pad_add_fusion.1.place_ref, s32[16,3]{1,0:T(8,128)S(1)} %bitcast.10, bf16[64,4,64,128]{3,2,1,0:T(8,128)(2,1)} %all_to_all.10.refs_0_.own_hbm, ...), custom_call_target="tpu_custom_call" | custom-call | flops 12884901888 | bytes 16777216 | tf_op jit(solution)/shard_map/attend_head/pallas_call | solution.py:251
  111.1 0.5 collective-permute-start.3
  111.5 3.8 %collective-permute-done.3.got_hbm = bf16[2,64,64,128]{3,2,1,0:T(8,128)(2,1)S(1)} collective-permute-done((bf16[2,64,64,128]{3,2,1,0:T(8,128)(2,1)S(1)}, bf16[2,64,64,128]{3,2,1,0:T(8,128)(2,1)S(1)}, u32[]{:S(2)}, u32[]{:S(2)}) %collective-permute-start.3) | collective-permute-done | bytes 2097184 | tf_op jit(solution)/shard_map/ppermute | solution.py:454
  115.3 1.1 combine_halves.1
  116.4 45.2 %all_to_all.11.refs_0_.source_ref = bf16[64,3,64,128]{3,2,1,0:T(8,128)(2,1)S(1)} all-to-all(bf16[64,3,64,128]{3,2,1,0:T(8,128)(2,1)S(1)} %combine_halves.1), channel_id=1, replica_groups=mesh['pipe'=2,'ctx'=16,'tp'=4] {'ctx','tp'}, dimensions={0} | all-to-all | bytes 6291456 | tf_op jit(solution)/shard_map/all_to_all | solution.py:456
  161.6 1.2 cut_heads.1
  162.8 2.2 %collective-permute-start.4 = (bf16[28,3,64,128]{3,2,1,0:T(8,128)(2,1)}, bf16[28,3,64,128]{3,2,1,0:T(8,128)(2,1)}, u32[]{:S(2)}, u32[]{:S(2)}) collective-permute-start(bf16[28,3,64,128]{3,2,1,0:T(8,128)(2,1)} %cut_heads.1), channel_id=1, source_target_pairs={{0,64},{64,0},{1,65},{65,1},{2,66},{66,2},{3,67},{67,3},{4,68},{68... | collective-permute-start | bytes 4128776 | tf_op jit(solution)/shard_map/ppermute | solution.py:464
  165.1 0.1 pad_add_fusion.2.place_ref
  165.2 0.1 pad_add_fusion.place_ref
  165.2 3.0 %gather_heads.2 = (bf16[1,128,3584]{2,1,0:T(8,128)(2,1)}, bf16[1,128,3584]{2,1,0:T(8,128)(2,1)}, bf16[1,128,3584]{2,1,0:T(8,128)(2,1)}, bf16[1,128,3584]{2,1,0:T(8,128)(2,1)}) custom-call(s32[2]{0:T(128)S(1)} %pad_add_fusion.2.place_ref, bf16[64,3,64,128]{3,2,1,0:T(8,128)(2,1)S(1)} %all_to_all.11.refs_0_.source_ref), custom_call_target="tpu_custom_call" | custom-call | bytes 4194304 | tf_op jit(solution)/shard_map/gather_heads/pallas_call | solution.py:379
  168.2 0.0 collective-permute-done.4.source_ref
  168.2 2.7 %gather_heads.3 = (bf16[1,128,3584]{2,1,0:T(8,128)(2,1)}, bf16[1,128,3584]{2,1,0:T(8,128)(2,1)}, bf16[1,128,3584]{2,1,0:T(8,128)(2,1)}, bf16[1,128,3584]{2,1,0:T(8,128)(2,1)}) custom-call(s32[2]{0:T(128)S(1)} %pad_add_fusion.place_ref, ...), custom_call_target="tpu_custom_call", output_to_operand_aliasing={{0}: (2, {}), {1}: (3, {}), {2}: (4, {}), {3}: (5, {})} | custom-call | bytes 4194304 | tf_op jit(solution)/shard_map/gather_heads/pallas_call | solution.py:379
  (1 shorter events, 0.0 us)
Async XLA Ops:
  0.6 3.9 %copy-start = (s32[1,16,3]{1,0,2:T(1,128)S(1)}, s32[1,16,3]{1,0,2:T(1,128)}, u32[]{:S(2)}) copy-start(s32[1,16,3]{1,0,2:T(1,128)} %param.9) | copy-start | bytes 580
  3.0 5.1 %collective-permute-start = (bf16[4,64,3584]{2,1,0:T(8,128)(2,1)}, bf16[4,64,3584]{2,1,0:T(8,128)(2,1)S(1)}, u32[]{:S(2)}, u32[]{:S(2)}) collective-permute-start(bf16[4,64,3584]{2,1,0:T(8,128)(2,1)} %cut_tokens.1), channel_id=1, source_target_pairs={{0,64},{64,0},{1,65},{65,1},{2,66},{66,2},{3,67},{67,3},{4,68},{68... | collective-permute-start | bytes 5505032 | tf_op jit(solution)/shard_map/ppermute | solution.py:435
  4.5 5.4 %collective-permute-start.1 = (s32[1,16,3]{1,0,2:T(1,128)S(1)}, s32[1,16,3]{1,0,2:T(1,128)S(1)}, u32[]{:S(2)}, u32[]{:S(2)}) collective-permute-start(s32[1,16,3]{1,0,2:T(1,128)S(1)} %copy-done), channel_id=1, source_target_pairs={{0,64},{64,0},{1,65},{65,1},{2,66},{66,2},{3,67},{67,3},{4,68},{68... | collective-permute-start | bytes 584 | tf_op jit(solution)/shard_map/ppermute | solution.py:436
  73.6 6.3 %collective-permute-start.2 = (bf16[64,2,64,128]{3,2,1,0:T(8,128)(2,1)S(1)}, bf16[64,2,64,128]{3,2,1,0:T(8,128)(2,1)}, u32[]{:S(2)}, u32[]{:S(2)}) collective-permute-start(bf16[64,2,64,128]{3,2,1,0:T(8,128)(2,1)S(1)} %cut_keys.1), channel_id=1, source_target_pairs={{0,64},{64,0},{1,65},{65,1},{2,66},{66,2},{3,67},{67,3},{4,68},{68... | collective-permute-start | bytes 6291464 | tf_op jit(solution)/shard_map/ppermute | solution.py:452
  111.1 4.2 %collective-permute-start.3 = (bf16[2,64,64,128]{3,2,1,0:T(8,128)(2,1)S(1)}, bf16[2,64,64,128]{3,2,1,0:T(8,128)(2,1)S(1)}, u32[]{:S(2)}, u32[]{:S(2)}) collective-permute-start(bf16[2,64,64,128]{3,2,1,0:T(8,128)(2,1)S(1)} %get-tuple-element.21), channel_id=1, source_target_pairs={{0,64},{64,0},{1,65},{65,1},{2,66},{66,2},{3,67},{67,3},{4,68},{68... | collective-permute-start | bytes 6291464 | tf_op jit(solution)/shard_map/ppermute | solution.py:454
  162.8 5.4 %collective-permute-start.4 = (bf16[28,3,64,128]{3,2,1,0:T(8,128)(2,1)}, bf16[28,3,64,128]{3,2,1,0:T(8,128)(2,1)}, u32[]{:S(2)}, u32[]{:S(2)}) collective-permute-start(bf16[28,3,64,128]{3,2,1,0:T(8,128)(2,1)} %cut_heads.1), channel_id=1, source_target_pairs={{0,64},{64,0},{1,65},{65,1},{2,66},{66,2},{3,67},{67,3},{4,68},{68... | collective-permute-start | bytes 4128776 | tf_op jit(solution)/shard_map/ppermute | solution.py:464

commit v7 on v5

--- a/solution.py
+++ b/solution.py
@@ -327,7 +327,8 @@
 
 def gather(core, source, base, high, results=None):
     heads = 4 * GROUP
-    groups = heads // GROUP
+    size = 4
+    groups = heads // size
     rows = slice(HALF, 2 * HALF) if high else slice(0, HALF)
 
     def kernel(place_ref, source_ref, *refs):
@@ -335,11 +336,11 @@
         got, cut, in_sem, out_sem = refs[-4:]
 
         def load(g):
-            at = pl.ds(place_ref[1] + g * GROUP, GROUP)
+            at = pl.ds(place_ref[1] + g * size, size)
             return pltpu.make_async_copy(source_ref.at[at], got.at[g], in_sem.at[g])
 
         def store(g, a):
-            cols = pl.ds(g * GROUP * HD, GROUP * HD)
+            cols = pl.ds(g * size * HD, size * HD)
             return pltpu.make_async_copy(cut.at[g, a], outs[a].at[0, rows, cols], out_sem.at[g, a])
 
         for g in range(groups):
@@ -348,7 +349,7 @@
             load(g).wait()
             for a in range(4):
                 live = place_ref[0] == (1 if a == 0 else 0)
-                for h in range(GROUP):
+                for h in range(size):
                     value = got[g, h, max(a - 1, 0)]
                     cut[g, a, :, h * HD : (h + 1) * HD] = jnp.where(live, value, jnp.zeros_like(value))
                 store(g, a).start()
@@ -360,8 +361,8 @@
     return call(
         kernel, "gather_heads", [jax.ShapeDtypeStruct((1, 2 * HALF, heads * HD), BF)] * 4, 1, 1 + len(extra),
         [
-            pltpu.VMEM((groups, GROUP, 3, HALF, HD), BF),
-            pltpu.VMEM((groups, 4, HALF, GROUP * HD), BF),
+            pltpu.VMEM((groups, size, 3, HALF, HD), BF),
+            pltpu.VMEM((groups, 4, HALF, size * HD), BF),
             pltpu.SemaphoreType.DMA((groups,)),
             pltpu.SemaphoreType.DMA((groups, 4)),
         ],

time: 171 us -> 173 us (1.012)
  transfers between devices with their start and end apart: 5 -> 5, of which waited for: 4 -> 3; matrix products, arithmetic and copies ran while one was open for 0% -> 0% of each run, Pallas kernels for 4% -> 5%
where the time goes in v7:
time: 173 us; the launch traced here: 172 us
  blocking collectives  107 us (62%)
  Pallas kernels  48.6 us (28%)
  waiting for transfers between devices  8.53 us (5%)
  starting transfers between devices  6.71 us (4%)
    all_to_all x1, blocking collectives, on_device(): own = lax.all_to_all(parts, CHIPS, 0, 0, tiled=True)  62 us
    all_to_all x1, blocking collectives, on_device(): back = lax.all_to_all(whole, CHIPS, 0, 0, tiled=True)  45.2 us
    pallas_call x1, Pallas kernels, attend(): call(attend_kernel, 'attend_head', [jax.ShapeDtypeStruct((n, 3, HALF, HD)...  31.1 us
    pallas_call x2, Pallas kernels, gather(): call(kernel, 'gather_heads', [jax.ShapeDtypeStruct((1, 2 * HALF, heads *...  6.9 us
    pallas_call x3, Pallas kernels, cut_out(): call(kernel, name, jax.ShapeDtypeStruct(out_shape, BF), 1, len(sources),...  5.16 us
    pallas_call x2, Pallas kernels, spread(): call(kernel, 'spread_heads', jax.ShapeDtypeStruct((2 * WIDE, 4, HALF, HD)...  4.29 us
    ppermute x1, waiting for transfers between devices, on_device(): whole = combine(first, mine, lax.ppermute(theirs, 'pipe', SWAP))  3.79 us
    ppermute x1, waiting for transfers between devices, on_device(): other = lax.ppermute(mine, 'pipe', SWAP)  3.75 us
  transfers between devices with their start and end apart: 5, of which 3 were waited for; matrix products, arithmetic and copies ran while one was open for 0% of the time, Pallas kernels for 5%

profile of v7, /device:TPU:1, one launch (start us, length us, event | category | flops | bytes accessed | tf_op | source)
XLA Modules:
  0.0 172.2 jit_solution(16195425404365569486)
XLA Ops:
  0.6 0.0 copy-start
  0.6 2.4 %cut_tokens.1 = bf16[4,64,3584]{2,1,0:T(8,128)(2,1)} custom-call(s32[1]{0:T(128)} %bitcast.place_ref, bf16[1,128,3584]{2,1,0:T(8,128)(2,1)} %refs_0_.1, bf16[1,128,3584]{2,1,0:T(8,128)(2,1)} %refs_1_.1, bf16[1,128,3584]{2,1,0:T(8,128)(2,1)} %refs_2_.1, bf16[1,128,3584]{2,1,0:T(8,128)(2,1)} %refs_3_.1), custom_call_target="tpu_custom_call" | custom-call | bytes 2097152 | tf_op jit(solution)/shard_map/cut_tokens/pallas_call | solution.py:392
  3.0 1.5 collective-permute-start
  4.5 0.0 copy-done
  4.5 0.1 collective-permute-start.1
  4.6 2.5 %spread_heads.2.refs_1_ = bf16[64,4,64,128]{3,2,1,0:T(8,128)(2,1)} custom-call(s32[1]{0:T(128)} %bitcast.place_ref, bf16[128,3584]{1,0:T(8,128)(2,1)} %bitcast.11, bf16[128,3584]{1,0:T(8,128)(2,1)} %bitcast.12, bf16[128,3584]{1,0:T(8,128)(2,1)} %bitcast.13, bf16[128,3584]{1,0:T(8,128)(2,1)} %bitcast.14), custom_call_target="tpu_custom_call" | custom-call | bytes 4194304 | tf_op jit(solution)/shard_map/spread_heads/pallas_call | solution.py:77
  7.1 1.0 collective-permute-done.refs_0_
  8.1 1.8 %spread_heads.3 = bf16[64,4,64,128]{3,2,1,0:T(8,128)(2,1)} custom-call(s32[1]{0:T(128)} %bitcast.3.place_ref, bf16[4,64,3584]{2,1,0:T(8,128)(2,1)S(1)} %collective-permute-done.refs_0_, bf16[64,4,64,128]{3,2,1,0:T(8,128)(2,1)} %spread_heads.2.refs_1_), custom_call_target="tpu_custom_call", output_to_operand_aliasing={{}: (2, {})} | custom-call | bytes 4194304 | tf_op jit(solution)/shard_map/spread_heads/pallas_call | solution.py:77
  9.9 0.0 collective-permute-done.1
  9.9 62.0 %all_to_all.10.refs_0_.own_hbm = bf16[64,4,64,128]{3,2,1,0:T(8,128)(2,1)} all-to-all(bf16[64,4,64,128]{3,2,1,0:T(8,128)(2,1)} %spread_heads.3), channel_id=1, replica_groups=mesh['pipe'=2,'ctx'=16,'tp'=4] {'ctx','tp'}, dimensions={0} | all-to-all | bytes 8388608 | tf_op jit(solution)/shard_map/all_to_all | solution.py:421
  72.0 1.6 cut_keys.1
  73.6 2.4 %collective-permute-start.2 = (bf16[64,2,64,128]{3,2,1,0:T(8,128)(2,1)S(1)}, bf16[64,2,64,128]{3,2,1,0:T(8,128)(2,1)}, u32[]{:S(2)}, u32[]{:S(2)}) collective-permute-start(bf16[64,2,64,128]{3,2,1,0:T(8,128)(2,1)S(1)} %cut_keys.1), channel_id=1, source_target_pairs={{0,64},{64,0},{1,65},{65,1},{2,66},{66,2},{3,67},{67,3},{4,68},{68... | collective-permute-start | bytes 6291464 | tf_op jit(solution)/shard_map/ppermute | solution.py:432
  76.0 0.1 pad_add_fusion.1.place_ref
  76.1 0.1 copy.16
  76.2 3.8 %collective-permute-done.2.other_hbm = bf16[64,2,64,128]{3,2,1,0:T(8,128)(2,1)} collective-permute-done((bf16[64,2,64,128]{3,2,1,0:T(8,128)(2,1)S(1)}, bf16[64,2,64,128]{3,2,1,0:T(8,128)(2,1)}, u32[]{:S(2)}, u32[]{:S(2)}) %collective-permute-start.2) | collective-permute-done | bytes 2097184 | tf_op jit(solution)/shard_map/ppermute | solution.py:432
  79.9 31.1 %attend_head.1 = (bf16[64,3,64,128]{3,2,1,0:T(8,128)(2,1)S(1)}, f32[2,64,64,128]{3,2,1,0:T(8,128)S(1)}, bf16[2,64,64,128]{3,2,1,0:T(8,128)(2,1)S(1)}) custom-call(s32[2]{0:T(128)S(1)} %pad_add_fusion.1.place_ref, s32[16,3]{1,0:T(8,128)S(1)} %bitcast.10, bf16[64,4,64,128]{3,2,1,0:T(8,128)(2,1)} %all_to_all.10.refs_0_.own_hbm, ...), custom_call_target="tpu_custom_call" | custom-call | flops 12884901888 | bytes 16777216 | tf_op jit(solution)/shard_map/attend_head/pallas_call | solution.py:251
  111.1 0.5 collective-permute-start.3
  111.5 3.8 %collective-permute-done.3.got_hbm = bf16[2,64,64,128]{3,2,1,0:T(8,128)(2,1)S(1)} collective-permute-done((bf16[2,64,64,128]{3,2,1,0:T(8,128)(2,1)S(1)}, bf16[2,64,64,128]{3,2,1,0:T(8,128)(2,1)S(1)}, u32[]{:S(2)}, u32[]{:S(2)}) %collective-permute-start.3) | collective-permute-done | bytes 2097184 | tf_op jit(solution)/shard_map/ppermute | solution.py:434
  115.3 1.1 combine_halves.1
  116.4 45.2 %all_to_all.11.refs_0_.source_ref = bf16[64,3,64,128]{3,2,1,0:T(8,128)(2,1)S(1)} all-to-all(bf16[64,3,64,128]{3,2,1,0:T(8,128)(2,1)S(1)} %combine_halves.1), channel_id=1, replica_groups=mesh['pipe'=2,'ctx'=16,'tp'=4] {'ctx','tp'}, dimensions={0} | all-to-all | bytes 6291456 | tf_op jit(solution)/shard_map/all_to_all | solution.py:436
  161.6 1.2 cut_heads.1
  162.8 2.2 %collective-permute-start.4 = (bf16[28,3,64,128]{3,2,1,0:T(8,128)(2,1)}, bf16[28,3,64,128]{3,2,1,0:T(8,128)(2,1)}, u32[]{:S(2)}, u32[]{:S(2)}) collective-permute-start(bf16[28,3,64,128]{3,2,1,0:T(8,128)(2,1)} %cut_heads.1), channel_id=1, source_target_pairs={{0,64},{64,0},{1,65},{65,1},{2,66},{66,2},{3,67},{67,3},{4,68},{68... | collective-permute-start | bytes 4128776 | tf_op jit(solution)/shard_map/ppermute | solution.py:444
  165.1 0.1 pad_add_fusion.2.place_ref
  165.2 0.1 pad_add_fusion.place_ref
  165.2 3.9 %gather_heads.2 = (bf16[1,128,3584]{2,1,0:T(8,128)(2,1)}, bf16[1,128,3584]{2,1,0:T(8,128)(2,1)}, bf16[1,128,3584]{2,1,0:T(8,128)(2,1)}, bf16[1,128,3584]{2,1,0:T(8,128)(2,1)}) custom-call(s32[2]{0:T(128)S(1)} %pad_add_fusion.2.place_ref, bf16[64,3,64,128]{3,2,1,0:T(8,128)(2,1)S(1)} %all_to_all.11.refs_0_.source_ref), custom_call_target="tpu_custom_call" | custom-call | bytes 4194304 | tf_op jit(solution)/shard_map/gather_heads/pallas_call | solution.py:361
  169.1 0.0 collective-permute-done.4.source_ref
  169.1 3.0 %gather_heads.3 = (bf16[1,128,3584]{2,1,0:T(8,128)(2,1)}, bf16[1,128,3584]{2,1,0:T(8,128)(2,1)}, bf16[1,128,3584]{2,1,0:T(8,128)(2,1)}, bf16[1,128,3584]{2,1,0:T(8,128)(2,1)}) custom-call(s32[2]{0:T(128)S(1)} %pad_add_fusion.place_ref, ...), custom_call_target="tpu_custom_call", output_to_operand_aliasing={{0}: (2, {}), {1}: (3, {}), {2}: (4, {}), {3}: (5, {})} | custom-call | bytes 4194304 | tf_op jit(solution)/shard_map/gather_heads/pallas_call | solution.py:361
  (1 shorter events, 0.0 us)
Async XLA Ops:
  0.6 3.9 %copy-start = (s32[1,16,3]{1,0,2:T(1,128)S(1)}, s32[1,16,3]{1,0,2:T(1,128)}, u32[]{:S(2)}) copy-start(s32[1,16,3]{1,0,2:T(1,128)} %param.9) | copy-start | bytes 580
  3.0 5.1 %collective-permute-start = (bf16[4,64,3584]{2,1,0:T(8,128)(2,1)}, bf16[4,64,3584]{2,1,0:T(8,128)(2,1)S(1)}, u32[]{:S(2)}, u32[]{:S(2)}) collective-permute-start(bf16[4,64,3584]{2,1,0:T(8,128)(2,1)} %cut_tokens.1), channel_id=1, source_target_pairs={{0,64},{64,0},{1,65},{65,1},{2,66},{66,2},{3,67},{67,3},{4,68},{68... | collective-permute-start | bytes 5505032 | tf_op jit(solution)/shard_map/ppermute | solution.py:415
  4.5 5.4 %collective-permute-start.1 = (s32[1,16,3]{1,0,2:T(1,128)S(1)}, s32[1,16,3]{1,0,2:T(1,128)S(1)}, u32[]{:S(2)}, u32[]{:S(2)}) collective-permute-start(s32[1,16,3]{1,0,2:T(1,128)S(1)} %copy-done), channel_id=1, source_target_pairs={{0,64},{64,0},{1,65},{65,1},{2,66},{66,2},{3,67},{67,3},{4,68},{68... | collective-permute-start | bytes 584 | tf_op jit(solution)/shard_map/ppermute | solution.py:416
  73.6 6.3 %collective-permute-start.2 = (bf16[64,2,64,128]{3,2,1,0:T(8,128)(2,1)S(1)}, bf16[64,2,64,128]{3,2,1,0:T(8,128)(2,1)}, u32[]{:S(2)}, u32[]{:S(2)}) collective-permute-start(bf16[64,2,64,128]{3,2,1,0:T(8,128)(2,1)S(1)} %cut_keys.1), channel_id=1, source_target_pairs={{0,64},{64,0},{1,65},{65,1},{2,66},{66,2},{3,67},{67,3},{4,68},{68... | collective-permute-start | bytes 6291464 | tf_op jit(solution)/shard_map/ppermute | solution.py:432
  111.1 4.2 %collective-permute-start.3 = (bf16[2,64,64,128]{3,2,1,0:T(8,128)(2,1)S(1)}, bf16[2,64,64,128]{3,2,1,0:T(8,128)(2,1)S(1)}, u32[]{:S(2)}, u32[]{:S(2)}) collective-permute-start(bf16[2,64,64,128]{3,2,1,0:T(8,128)(2,1)S(1)} %get-tuple-element.21), channel_id=1, source_target_pairs={{0,64},{64,0},{1,65},{65,1},{2,66},{66,2},{3,67},{67,3},{4,68},{68... | collective-permute-start | bytes 6291464 | tf_op jit(solution)/shard_map/ppermute | solution.py:434
  162.8 6.3 %collective-permute-start.4 = (bf16[28,3,64,128]{3,2,1,0:T(8,128)(2,1)}, bf16[28,3,64,128]{3,2,1,0:T(8,128)(2,1)}, u32[]{:S(2)}, u32[]{:S(2)}) collective-permute-start(bf16[28,3,64,128]{3,2,1,0:T(8,128)(2,1)} %cut_heads.1), channel_id=1, source_target_pairs={{0,64},{64,0},{1,65},{65,1},{2,66},{66,2},{3,67},{67,3},{4,68},{68... | collective-permute-start | bytes 4128776 | tf_op jit(solution)/shard_map/ppermute | solution.py:444
